TPU v7x, 512 devices: a whole 4x8x8 slice. The times are simulated.
512 devices in a mesh: row: 16 (over y_lo, x, core), col: 32 (over z, y_hi).
Axes of the slice: x: 4, y: 8 (y_hi: 4, y_lo: 2; y = y_hi * 2 + y_lo), z: 8, core: 2. Of those that a mesh axis runs over, the one named last changes fastest.
Arguments:
- panel: bfloat16 [16, 32, 128, 512], P('row', 'col'), may hold values from -6 to 6
- blocks: bfloat16 [16, 32, 128, 128, 128], P('row', 'col'), may hold values from -0.0625 to 0.0625
- block_rows: int32 [16, 32, 128], P('row', 'col'), may hold values from 0 to 31
- block_cols: int32 [16, 32, 128], P('row', 'col'), may hold values from 0 to 15
- block_count: int32 [16, 32], P('row', 'col'), may hold values from 16 to 128, as said below
- pre_act: bfloat16 [32, 16, 128, 512], P('col', 'row'), may hold values from -6 to 6
Outputs:
- grad_input: bfloat16 [32, 16, 128, 512], P('col', 'row')
Inputs may be any that keep to these rules, and one draw needn't show every extreme that they name: `block_count`: some device has exactly 128 live slots and some exactly 16; counts are 128 divided by 1, 2, 4 or 8.
All inputs are finite; a program needn't handle non-finite values.
Results may differ from a plain program's by a relative error of at most 0.015.
Values may be sent and summed in bfloat16 or wider, within the bound.
No kernel may reach another device: no remote copies, remote signals or barrier semaphores. Data moves between devices by JAX's collectives and lax.ppermute only.
A program may use at most 128 MiB of HBM per device.

v0:
```python
import jax
import jax.numpy as jnp
from jax import lax
from jax.sharding import PartitionSpec as P

GROUP = 16


def block_products(total, values, rows, cols, lower, upper, source, offset):
    lower = jnp.maximum(lower, 0)
    upper = jnp.maximum(upper, lower)
    last_row = source.shape[0] - 1

    def group_step(index, total):
        start = index * GROUP
        vals = lax.dynamic_slice_in_dim(values, start, GROUP, 0)
        row_sel = lax.dynamic_slice_in_dim(rows, start, GROUP, 0)
        col_sel = lax.dynamic_slice_in_dim(cols, start, GROUP, 0)
        slot = start + lax.iota(jnp.int32, GROUP)
        live = (slot >= lower) & (slot < upper)
        local_rows = jnp.clip(row_sel - offset, 0, last_row)
        picked = jnp.take(source, local_rows, axis=0)
        prod = jnp.einsum("bij,bif->bjf", vals, picked, preferred_element_type=jnp.float32)
        prod = jnp.where(live[:, None, None], prod, jnp.float32(0.0))
        return total.at[col_sel].add(prod)

    return lax.fori_loop(lower // GROUP, (upper + GROUP - 1) // GROUP, group_step, total)


def run_panel(panel, work_sets, empty):
    whole = lax.all_gather(panel, "col", axis=1, tiled=True)[0]
    return tuple(
        (
            block_products(empty, vals, rws, cls, low, high, whole, 0)
            for vals, rws, cls, low, high in work_sets
        )
    )


def shards(panel, blocks, block_rows, block_cols, block_count, pre_act):
    values = blocks[0, 0]
    rows = block_rows[0, 0]
    cols = block_cols[0, 0]
    count = block_count[0, 0]
    cols_dev = pre_act.shape[1] * lax.axis_size("row")
    empty = jnp.zeros((cols_dev, panel.shape[2], panel.shape[3]), jnp.float32)
    results = run_panel(panel, [(values, rows, cols, 0, count)], empty)
    total = results[0]
    share = lax.psum_scatter(total, "row", scatter_dimension=0, tiled=True)
    result = jnp.where(pre_act[0] > 0, share, jnp.float32(0.0))
    return result.astype(jnp.bfloat16)[None]


def solution(mesh):
    placed = (
        P("row", "col", None, None),
        P("row", "col", None, None, None),
        P("row", "col", None),
        P("row", "col", None),
        P("row", "col"),
        P("col", "row", None, None),
    )
    return jax.shard_map(
        shards, mesh=mesh, in_specs=placed, out_specs=P("col", "row", None, None), check_vma=False
    )
```

profile of v0, /device:TPU:16, one launch (start us, length us, event | category | flops | bytes accessed | tf_op | source)
XLA Modules:
  0.0 326.0 jit_solution(10697834047759395783)
XLA Ops:
  6.5 0.0 all-gather.2.cloned.1.call-start
  6.5 0.7 all-gather.2.cloned.1.call-update
  7.3 0.0 reduce-scatter.2.cloned.1.call-start
  8.0 6.4 %copy.8 = bf16[1,1,128,128,128]{3,4,2,1,0:T(8,128)(2,1)} copy(bf16[1,1,128,128,128]{4,3,2,1,0:T(8,128)(2,1)} %param.9) | data formatting | bytes 8388608 | tf_op args[1]
  14.4 101.8 %all-gather.2.cloned.1.call-done = bf16[1,32,128,512]{3,2,0,1:T(8,128)(2,1)} async-done(((bf16[1,1,128,512]{3,2,0,1:T(8,128)(2,1)}), bf16[1,32,128,512]{3,2,0,1:T(8,128)(2,1)}) %all-gather.2.cloned.1.call-update) | async-done | bytes 4194320 | tf_op jit(solution)/shard_map/all_gather | solution.py:31
  116.2 2.5 broadcast_in_dim.38
  118.7 0.0 copy-done.1
  118.7 65.0 %while.10 = (s32[]{:T(128)}, f32[16,128,512]{2,1,0:T(8,128)}, s32[]{:T(128)}, s32[128]{0:T(128)S(1)}, s32[]{:T(128)}, /*index=5*/bf16[128,128,128]{1,2,0:T(8,128...) while((s32[]{:T(128)}, f32[16,128,512]{2,1,0:T(8,128)}, ...), condition=%wide.region_2.3_spmd, body=%wide.region_0.2_spmd.sunk | while | flops 271582432 | bytes 23597752 | solution.py:27
  118.7 0.1 compare_select_fusion.4
  118.8 0.1 compare_and_fusion.3
  118.8 2.9 gather_fusion
  121.7 3.8 %convolution_select_fusion.2 = f32[16,128,512]{2,1,0:T(8,128)} fusion(bf16[16,128,512]{2,1,0:T(8,128)(2,1)S(1)} %gather_fusion, pred[16]{0:T(512)(128)(4,1)S(1)} %get-tuple-element.122, pred[16]{0:T(512)(128)(4,1)S(1)} %get-tuple-element.123, bf16[128,128,128]{1,2,0:T(8,128)(2,1)} %get-tuple-element.153, s32[]{:T(128)S(6)} %select_n.51), kind=kOutput, calls=%fused_computation.2.clone.1 | convolution fusion | flops 270532608 | bytes 6815780 | tf_op jit(solution)/shard_map/while/body/bij,bif->bjf/dot_general | solution.py:23
  125.5 9.3 %scatter_fusion = f32[16,128,512]{2,1,0:T(8,128)} fusion(f32[16,128,512]{2,1,0:T(8,128)} %get-tuple-element.137, s32[16]{0:T(128)S(1)} %compare_select_fusion.4, f32[16,128,512]{2,1,0:T(8,128)} %convolution_select_fusion.2), kind=kCustom, calls=%fused_computation.1.clone.1 | custom fusion | flops 1048576 | bytes 12582976 | tf_op jit(solution)/shard_map/while/body/scatter-add | solution.py:25
  134.8 0.1 compare_select_fusion.4
  134.9 0.1 compare_and_fusion.3
  135.0 2.9 gather_fusion
  137.9 3.8 %convolution_select_fusion.2 = f32[16,128,512]{2,1,0:T(8,128)} fusion(bf16[16,128,512]{2,1,0:T(8,128)(2,1)S(1)} %gather_fusion, pred[16]{0:T(512)(128)(4,1)S(1)} %get-tuple-element.122, pred[16]{0:T(512)(128)(4,1)S(1)} %get-tuple-element.123, bf16[128,128,128]{1,2,0:T(8,128)(2,1)} %get-tuple-element.153, s32[]{:T(128)S(6)} %select_n.51), kind=kOutput, calls=%fused_computation.2.clone.1 | convolution fusion | flops 270532608 | bytes 6815780 | tf_op jit(solution)/shard_map/while/body/bij,bif->bjf/dot_general | solution.py:23
  141.7 9.4 %scatter_fusion = f32[16,128,512]{2,1,0:T(8,128)} fusion(f32[16,128,512]{2,1,0:T(8,128)} %get-tuple-element.137, s32[16]{0:T(128)S(1)} %compare_select_fusion.4, f32[16,128,512]{2,1,0:T(8,128)} %convolution_select_fusion.2), kind=kCustom, calls=%fused_computation.1.clone.1 | custom fusion | flops 1048576 | bytes 12582976 | tf_op jit(solution)/shard_map/while/body/scatter-add | solution.py:25
  151.1 0.1 compare_select_fusion.4
  151.2 0.1 compare_and_fusion.3
  151.3 2.9 gather_fusion
  154.1 3.8 %convolution_select_fusion.2 = f32[16,128,512]{2,1,0:T(8,128)} fusion(bf16[16,128,512]{2,1,0:T(8,128)(2,1)S(1)} %gather_fusion, pred[16]{0:T(512)(128)(4,1)S(1)} %get-tuple-element.122, pred[16]{0:T(512)(128)(4,1)S(1)} %get-tuple-element.123, bf16[128,128,128]{1,2,0:T(8,128)(2,1)} %get-tuple-element.153, s32[]{:T(128)S(6)} %select_n.51), kind=kOutput, calls=%fused_computation.2.clone.1 | convolution fusion | flops 270532608 | bytes 6815780 | tf_op jit(solution)/shard_map/while/body/bij,bif->bjf/dot_general | solution.py:23
  157.9 9.6 %scatter_fusion = f32[16,128,512]{2,1,0:T(8,128)} fusion(f32[16,128,512]{2,1,0:T(8,128)} %get-tuple-element.137, s32[16]{0:T(128)S(1)} %compare_select_fusion.4, f32[16,128,512]{2,1,0:T(8,128)} %convolution_select_fusion.2), kind=kCustom, calls=%fused_computation.1.clone.1 | custom fusion | flops 1048576 | bytes 12582976 | tf_op jit(solution)/shard_map/while/body/scatter-add | solution.py:25
  167.5 0.1 compare_select_fusion.4
  167.6 0.1 compare_and_fusion.3
  167.7 2.9 gather_fusion
  170.5 3.8 %convolution_select_fusion.2 = f32[16,128,512]{2,1,0:T(8,128)} fusion(bf16[16,128,512]{2,1,0:T(8,128)(2,1)S(1)} %gather_fusion, pred[16]{0:T(512)(128)(4,1)S(1)} %get-tuple-element.122, pred[16]{0:T(512)(128)(4,1)S(1)} %get-tuple-element.123, bf16[128,128,128]{1,2,0:T(8,128)(2,1)} %get-tuple-element.153, s32[]{:T(128)S(6)} %select_n.51), kind=kOutput, calls=%fused_computation.2.clone.1 | convolution fusion | flops 270532608 | bytes 6815780 | tf_op jit(solution)/shard_map/while/body/bij,bif->bjf/dot_general | solution.py:23
  174.3 9.3 %scatter_fusion = f32[16,128,512]{2,1,0:T(8,128)} fusion(f32[16,128,512]{2,1,0:T(8,128)} %get-tuple-element.137, s32[16]{0:T(128)S(1)} %compare_select_fusion.4, f32[16,128,512]{2,1,0:T(8,128)} %convolution_select_fusion.2), kind=kCustom, calls=%fused_computation.1.clone.1 | custom fusion | flops 1048576 | bytes 12582976 | tf_op jit(solution)/shard_map/while/body/scatter-add | solution.py:25
  183.6 0.0 reduce-scatter.2.cloned.1.call-update
  183.7 133.8 %reduce-scatter.2.cloned.1.call-done = f32[1,128,512]{2,1,0:T(8,128)} async-done(((f32[16,128,512]{2,1,0:T(8,128)}), f32[1,128,512]{2,1,0:T(8,128)}) %reduce-scatter.2.cloned.1.call-update) | async-done | bytes 262160 | tf_op jit(solution)/shard_map/reduce_scatter | solution.py:49
  317.5 0.0 copy-done
  317.5 1.6 fusion.6
  (8 shorter events, 0.0 us)
Async XLA Ops:
  6.5 109.7 %all-gather.2.cloned.1.call-start = ((), (), s32[]{:S(2)}) async-start(), calls=%async_computation.1 | async-start | bytes 4325376 | tf_op jit(solution)/shard_map/all_gather | solution.py:31
  7.3 310.2 %reduce-scatter.2.cloned.1.call-start = ((), (), s32[]{:S(2)}) async-start(), calls=%async_computation.2 | async-start | bytes 4456448 | tf_op jit(solution)/shard_map/reduce_scatter | solution.py:49
  14.4 104.3 %copy-start.1 = (s32[1,1,128]{2,1,0:T(1,128)S(1)}, s32[1,1,128]{2,1,0:T(1,128)}, u32[]{:S(2)}) copy-start(s32[1,1,128]{2,1,0:T(1,128)} %param.10) | copy-start | bytes 1540
  14.4 104.3 %copy-start.2 = (s32[1,1,128]{2,1,0:T(1,128)S(1)}, s32[1,1,128]{2,1,0:T(1,128)}, u32[]{:S(2)}) copy-start(s32[1,1,128]{2,1,0:T(1,128)} %param.11) | copy-start | bytes 1540
  183.6 133.8 %copy-start = (bf16[1,1,128,512]{3,2,1,0:T(8,128)(2,1)S(1)}, bf16[1,1,128,512]{3,2,1,0:T(8,128)(2,1)}, u32[]{:S(2)}) copy-start(bf16[1,1,128,512]{3,2,1,0:T(8,128)(2,1)} %param.13) | copy-start | bytes 393220
Sparse Core Ops, SparseCore 0:
  10.5 105.6 all-gather.1
  183.8 133.6 reduce-scatter.1
where the time goes:
time: 327 us; the launch traced here: 326 us
  waiting for transfers between devices  236 us (72%)
  other arithmetic  40 us (12%)
  local copies, waits for them, and re-layouts  20.4 us (6%)
  matrix products  15.1 us (5%)
  between operations  14.1 us (4%)
    reduce_scatter x1, waiting for transfers between devices, shards(): share = lax.psum_scatter(total, 'row', scatter_dimension=0, tiled=True)  134 us
    all_gather x1, waiting for transfers between devices, run_panel(): whole = lax.all_gather(panel, 'col', axis=1, tiled=True)[0]  102 us
    scatter-add x4, other arithmetic, group_step(): return total.at[col_sel].add(prod)  37.7 us
    dot_general x4, matrix products, group_step(): jnp.einsum('bij,bif->bjf', vals, picked, preferred_element_type=jnp.float32)  15.1 us
    gather x4, local copies, waits for them, and re-layouts, group_step(): picked = jnp.take(source, local_rows, axis=0)  11.5 us
  transfers between devices with their start and end apart: 2, of which 2 were waited for; matrix products, arithmetic and copies ran while one was open for 2% of the time, Pallas kernels for 0%

commit v1 on v0

v1 whole, which is shorter than its diff:
```python
import functools
import itertools

import jax
import jax.numpy as jnp
from jax import lax
from jax.experimental import pallas as pl
from jax.experimental.pallas import tpu as pltpu
from jax.sharding import PartitionSpec as P

YL, X, CORE, Z, YH = 2, 4, 2, 8, 4
AXES = ("row", "col")
GROUP = 16
PARTS = 2


def place(yl, x, core, z, yh):
    row = ((yl % YL) * X + x % X) * CORE + core % CORE
    return row * (Z * YH) + (z % Z) * YH + yh % YH


def moves(step):
    spots = itertools.product(range(YL), range(X), range(CORE), range(Z), range(YH))
    return [(place(*spot), place(*step(*spot))) for spot in spots]


def along_y(by):
    return lambda yl, x, core, z, yh: (yl, x, core, z, yh + by)


def along_z(by):
    return lambda yl, x, core, z, yh: (yl, x, core, z + by, yh)


def other_core(yl, x, core, z, yh):
    return yl, x, core + 1, z, yh


def send(value, step):
    return lax.ppermute(value, AXES, moves(step))


def spmm_kernel(first, meta, blocks, *refs):
    pieces = refs[:-7]
    keep, away, vals, pan, acc, piece_sem, block_sem = refs[-7:]
    sizes = [piece.shape[0] for piece in pieces]
    starts = [sum(sizes[:k]) for k in range(len(sizes))]
    slots = blocks.shape[0]
    count = meta[2 * slots]
    core = meta[2 * slots + 1]
    groups = count // GROUP

    def block_copy(g):
        part = pl.ds(g * GROUP, GROUP)
        return pltpu.make_async_copy(blocks.at[part], vals.at[part], block_sem.at[g])

    def piece_copy(k):
        part = pieces[k].at[:, :, pl.ds(first, pan.shape[2])]
        return pltpu.make_async_copy(part, pan.at[pl.ds(starts[k], sizes[k])], piece_sem.at[k])

    block_copy(0).start()
    for k in range(len(pieces)):
        piece_copy(k).start()

    @pl.loop(1, groups)
    def _(g):
        block_copy(g).start()

    acc[...] = jnp.zeros_like(acc)
    for k in range(len(pieces)):
        piece_copy(k).wait()

    @pl.loop(0, groups)
    def _(g):
        block_copy(g).wait()
        for s in range(GROUP):
            slot = g * GROUP + s
            prod = lax.dot_general(
                vals[slot], pan[meta[slot]], (((0,), (0,)), ((), ())), preferred_element_type=jnp.float32
            )
            col = meta[slots + slot]
            acc[col] = acc[col] + prod

    for k in range(keep.shape[0]):
        keep[k] = acc[CORE * k + core]
        away[k] = acc[CORE * k + 1 - core].astype(away.dtype)


def spmm(meta, values, pieces, first, width):
    slots, bs = values.shape[0], values.shape[1]
    blocks_out = YL * X
    anywhere = pl.BlockSpec(memory_space=pl.ANY)
    return pl.pallas_call(
        functools.partial(spmm_kernel, first),
        out_shape=(
            jax.ShapeDtypeStruct((blocks_out, bs, width), jnp.float32),
            jax.ShapeDtypeStruct((blocks_out, bs, width), jnp.bfloat16),
        ),
        in_specs=[pl.BlockSpec(memory_space=pltpu.SMEM), pl.BlockSpec(memory_space=pltpu.HBM)]
        + [anywhere] * len(pieces),
        out_specs=[pl.BlockSpec(memory_space=pltpu.VMEM)] * 2,
        scratch_shapes=[
            pltpu.VMEM(values.shape, jnp.bfloat16),
            pltpu.VMEM((Z * YH, bs, width), jnp.bfloat16),
            pltpu.VMEM((blocks_out * CORE, bs, width), jnp.float32),
            pltpu.SemaphoreType.DMA((len(pieces),)),
            pltpu.SemaphoreType.DMA((slots // GROUP,)),
        ],
        compiler_params=pltpu.CompilerParams(vmem_limit_bytes=32 * 2**20),
        cost_estimate=pl.CostEstimate(
            flops=2 * slots * bs * bs * width, bytes_accessed=8 * 2**20, transcendentals=0
        ),
    )(meta, values, *pieces)


def combine_kernel(keep, came, out):
    out[...] = (keep[...] + came[...].astype(jnp.float32)).astype(out.dtype)


def combine(keep, came):
    whole = pl.BlockSpec(memory_space=pltpu.VMEM)
    return pl.pallas_call(
        combine_kernel,
        out_shape=jax.ShapeDtypeStruct(keep.shape, jnp.bfloat16),
        in_specs=[whole, whole],
        out_specs=whole,
        compiler_params=pltpu.CompilerParams(vmem_limit_bytes=16 * 2**20),
        cost_estimate=pl.CostEstimate(flops=keep.size, bytes_accessed=8 * keep.size, transcendentals=0),
    )(keep, came)


def finish_kernel(pre, *refs):
    out = refs[-1]
    width = pre.shape[1] // PARTS
    for part in range(PARTS):
        terms = refs[part]
        total = terms[0].astype(jnp.float32)
        for k in range(1, YL * X):
            total = total + terms[k].astype(jnp.float32)
        cols = slice(part * width, (part + 1) * width)
        gate = pre[:, cols].astype(jnp.float32) > 0
        out[:, cols] = jnp.where(gate, total, 0.0).astype(out.dtype)


def finish(pre, terms):
    whole = pl.BlockSpec(memory_space=pltpu.VMEM)
    return pl.pallas_call(
        finish_kernel,
        out_shape=jax.ShapeDtypeStruct(pre.shape, jnp.bfloat16),
        in_specs=[whole] * (1 + len(terms)),
        out_specs=whole,
        compiler_params=pltpu.CompilerParams(vmem_limit_bytes=16 * 2**20),
        cost_estimate=pl.CostEstimate(flops=9 * pre.size, bytes_accessed=20 * pre.size, transcendentals=0),
    )(pre, *terms)


def gather_column(part):
    return [part, send(part, along_y(1)), send(part, along_y(2)), send(part, along_y(-1))]


def gather_rings(mine):
    low, high = [mine], [mine]
    for _ in range(Z // 2 - 1):
        low.append(send(low[-1], along_z(1)))
        high.append(send(high[-1], along_z(-1)))
    cut = YH // 2
    middle = [send(low[-1][:cut], along_z(1)), send(high[-1][cut:], along_z(-1))]
    return low + middle + high[:0:-1]


def reduce_part(keep, away):
    both = combine(keep, send(away, other_core))
    groups = [[CORE * k + core for k in range(YL * X)] for core in range(CORE)]
    return lax.all_to_all(both, "row", 0, 0, axis_index_groups=groups, tiled=True)


def shards(panel, blocks, block_rows, block_cols, block_count, pre_act):
    values = blocks[0, 0]
    col = lax.axis_index("col")
    core = (lax.axis_index("row") & 1).astype(jnp.int32)
    z, yh = col >> 2, col & (YH - 1)
    rows = block_rows[0, 0]
    near = ((z - (rows >> 2)) & (Z - 1)) * YH + ((yh - rows) & (YH - 1))
    meta = jnp.concatenate([near, block_cols[0, 0], block_count[0], core[None]])

    width = panel.shape[3] // PARTS
    column = gather_column(panel[0, 0])
    pieces = gather_rings(jnp.stack(column))
    parts = [spmm(meta, values, pieces, p * width, width) for p in range(PARTS)]
    terms = [reduce_part(*part) for part in parts]
    return finish(pre_act[0, 0], terms)[None, None]


def solution(mesh):
    placed = (
        P("row", "col", None, None),
        P("row", "col", None, None, None),
        P("row", "col", None),
        P("row", "col", None),
        P("row", "col"),
        P("col", "row", None, None),
    )
    return jax.shard_map(
        shards, mesh=mesh, in_specs=placed, out_specs=P("col", "row", None, None), check_vma=False
    )
```

time: 327 us -> 138 us (0.42)
  waiting for transfers between devices: 236 us -> 39.1 us
  starting transfers between devices: 0.04 us -> 61.1 us
  other arithmetic: 40 us -> 2.36 us
  blocking collectives: 0 us -> 17.7 us
  matrix products: 15.1 us -> 0 us
  local copies, waits for them, and re-layouts: 20.4 us -> 6.25 us
  between operations: 14.1 us -> 0.87 us
  Pallas kernels: 0 us -> 9.71 us
    reduce_scatter x1 -> x0, waiting for transfers between devices: 134 us -> none  [shards(): share = lax.psum_scatter(total, 'row', scatter_dimension=0, tiled=True)]
    all_gather x1 -> x0, waiting for transfers between devices: 102 us -> none  [run_panel(): whole = lax.all_gather(panel, 'col', axis=1, tiled=True)[0]]
    ppermute x0 -> x13, starting transfers between devices: none -> 51 us  [send(): return lax.ppermute(value, AXES, moves(step))]
    ppermute x0 -> x13, waiting for transfers between devices: none -> 39.1 us  [send(): return lax.ppermute(value, AXES, moves(step))]
    scatter-add x4 -> x0, other arithmetic: 37.7 us -> none  [group_step(): return total.at[col_sel].add(prod)]
    all_to_all x0 -> x1, blocking collectives: none -> 17.7 us  [reduce_part(): lax.all_to_all(both, 'row', 0, 0, axis_index_groups=groups, tiled=True)]
    dot_general x4 -> x0, matrix products: 15.1 us -> none  [group_step(): jnp.einsum('bij,bif->bjf', vals, picked, preferred_element_type=jnp.float32)]
    gather x4 -> x0, local copies, waits for them, and re-layouts: 11.5 us -> none  [group_step(): picked = jnp.take(source, local_rows, axis=0)]
  transfers between devices with their start and end apart: 2 -> 14, of which waited for: 2 -> 9; matrix products, arithmetic and copies ran while one was open for 2% -> 1% of each run, Pallas kernels for 0% -> 3%
where the time goes in v1:
time: 138 us; the launch traced here: 137 us
  starting transfers between devices  61.1 us (44%)
  waiting for transfers between devices  39.1 us (28%)
  blocking collectives  17.7 us (13%)
  Pallas kernels  9.71 us (7%)
  local copies, waits for them, and re-layouts  6.25 us (5%)
  other arithmetic  2.36 us (2%)
    ppermute x13, starting transfers between devices, send(): return lax.ppermute(value, AXES, moves(step))  51 us
    ppermute x13, waiting for transfers between devices, send(): return lax.ppermute(value, AXES, moves(step))  39.1 us
    all_to_all x1, blocking collectives, reduce_part(): lax.all_to_all(both, 'row', 0, 0, axis_index_groups=groups, tiled=True)  17.7 us
    all_to_all x1, starting transfers between devices, reduce_part(): lax.all_to_all(both, 'row', 0, 0, axis_index_groups=groups, tiled=True)  10.1 us
    pallas_call x2, Pallas kernels, spmm(): pl.pallas_call(functools.partial(spmm_kernel, first), out_shape=(jax.Shap...  7.68 us
    unnamed x12, local copies, waits for them, and re-layouts  6.21 us
  transfers between devices with their start and end apart: 14, of which 9 were waited for; matrix products, arithmetic and copies ran while one was open for 1% of the time, Pallas kernels for 3%

profile of v1, /device:TPU:16, one launch (start us, length us, event | category | flops | bytes accessed | tf_op | source)
XLA Modules:
  0.0 137.1 jit_solution(7995867642084411872)
XLA Ops:
  0.0 7.6 %collective-permute-start.2 = (bf16[128,512]{1,0:T(8,128)(2,1)}, bf16[128,512]{1,0:T(8,128)(2,1)S(1)}, u32[]{:S(2)}, u32[]{:S(2)}) collective-permute-start(bf16[128,512]{1,0:T(8,128)(2,1)} %bitcast.17), channel_id=1, source_target_pairs={{0,3},{1,0},{2,1},{3,2},{4,7},{5,4},{6,5},{7,6},{8,11},{9,8},{10,9... | collective-permute-start | bytes 393224 | tf_op jit(solution)/shard_map/ppermute | solution.py:40
  7.6 2.4 %collective-permute-start.1 = (bf16[128,512]{1,0:T(8,128)(2,1)}, bf16[128,512]{1,0:T(8,128)(2,1)S(1)}, u32[]{:S(2)}, u32[]{:S(2)}) collective-permute-start(bf16[128,512]{1,0:T(8,128)(2,1)} %bitcast.18), channel_id=1, source_target_pairs={{0,2},{1,3},{2,0},{3,1},{4,6},{5,7},{6,4},{7,5},{8,10},{9,11},{10,... | collective-permute-start | bytes 393224 | tf_op jit(solution)/shard_map/ppermute | solution.py:40
  10.0 5.0 %collective-permute-start = (bf16[128,512]{1,0:T(8,128)(2,1)}, bf16[128,512]{1,0:T(8,128)(2,1)S(1)}, u32[]{:S(2)}, u32[]{:S(2)}) collective-permute-start(bf16[128,512]{1,0:T(8,128)(2,1)} %bitcast.19), channel_id=1, source_target_pairs={{0,1},{1,2},{2,3},{3,0},{4,5},{5,6},{6,7},{7,4},{8,9},{9,10},{10,1... | collective-permute-start | bytes 393224 | tf_op jit(solution)/shard_map/ppermute | solution.py:40
  15.0 5.2 %collective-permute-done.1 = bf16[128,512]{1,0:T(8,128)(2,1)S(1)} collective-permute-done((bf16[128,512]{1,0:T(8,128)(2,1)}, bf16[128,512]{1,0:T(8,128)(2,1)S(1)}, u32[]{:S(2)}, u32[]{:S(2)}) %collective-permute-start.1) | collective-permute-done | bytes 131104 | tf_op jit(solution)/shard_map/ppermute | solution.py:40
  20.2 1.0 collective-permute-done
  21.2 1.0 pad_maximum_fusion.refs_0_
  22.2 2.4 %collective-permute-start.3 = (bf16[4,128,512]{2,1,0:T(8,128)(2,1)S(1)}, bf16[4,128,512]{2,1,0:T(8,128)(2,1)S(1)}, u32[]{:S(2)}, u32[]{:S(2)}) collective-permute-start(bf16[4,128,512]{2,1,0:T(8,128)(2,1)S(1)} %pad_maximum_fusion.refs_0_), channel_id=1, source_target_pairs={{0,4},{1,5},{2,6},{3,7},{4,8},{5,9},{6,10},{7,11},{8,12},{9,13},{1... | collective-permute-start | bytes 1572872 | tf_op jit(solution)/shard_map/ppermute | solution.py:40
  24.6 8.6 %collective-permute-start.7 = (bf16[4,128,512]{2,1,0:T(8,128)(2,1)S(1)}, bf16[4,128,512]{2,1,0:T(8,128)(2,1)S(1)}, u32[]{:S(2)}, u32[]{:S(2)}) collective-permute-start(bf16[4,128,512]{2,1,0:T(8,128)(2,1)S(1)} %pad_maximum_fusion.refs_0_), channel_id=1, source_target_pairs={{0,28},{1,29},{2,30},{3,31},{4,0},{5,1},{6,2},{7,3},{8,4},{9,5},{1... | collective-permute-start | bytes 1572872 | tf_op jit(solution)/shard_map/ppermute | solution.py:40
  33.2 10.0 %collective-permute-done.3.refs_1_ = bf16[4,128,512]{2,1,0:T(8,128)(2,1)S(1)} collective-permute-done((bf16[4,128,512]{2,1,0:T(8,128)(2,1)S(1)}, bf16[4,128,512]{2,1,0:T(8,128)(2,1)S(1)}, u32[]{:S(2)}, u32[]{:S(2)}) %collective-permute-start.3) | collective-permute-done | bytes 524320 | tf_op jit(solution)/shard_map/ppermute | solution.py:40
  43.2 1.9 %collective-permute-start.4 = (bf16[4,128,512]{2,1,0:T(8,128)(2,1)S(1)}, bf16[4,128,512]{2,1,0:T(8,128)(2,1)S(1)}, u32[]{:S(2)}, u32[]{:S(2)}) collective-permute-start(bf16[4,128,512]{2,1,0:T(8,128)(2,1)S(1)} %collective-permute-done.3.refs_1_), channel_id=1, source_target_pairs={{0,4},{1,5},{2,6},{3,7},{4,8},{5,9},{6,10},{7,11},{8,12},{9,13},{1... | collective-permute-start | bytes 1572872 | tf_op jit(solution)/shard_map/ppermute | solution.py:40
  45.1 5.1 %collective-permute-start.8 = (bf16[4,128,512]{2,1,0:T(8,128)(2,1)S(1)}, bf16[4,128,512]{2,1,0:T(8,128)(2,1)}, u32[]{:S(2)}, u32[]{:S(2)}) collective-permute-start(bf16[4,128,512]{2,1,0:T(8,128)(2,1)S(1)} %collective-permute-done.7.refs_8_), channel_id=1, source_target_pairs={{0,28},{1,29},{2,30},{3,31},{4,0},{5,1},{6,2},{7,3},{8,4},{9,5},{1... | collective-permute-start | bytes 1572872 | tf_op jit(solution)/shard_map/ppermute | solution.py:40
  50.3 9.1 %collective-permute-done.4.refs_2_ = bf16[4,128,512]{2,1,0:T(8,128)(2,1)S(1)} collective-permute-done((bf16[4,128,512]{2,1,0:T(8,128)(2,1)S(1)}, bf16[4,128,512]{2,1,0:T(8,128)(2,1)S(1)}, u32[]{:S(2)}, u32[]{:S(2)}) %collective-permute-start.4) | collective-permute-done | bytes 524320 | tf_op jit(solution)/shard_map/ppermute | solution.py:40
  59.4 1.9 %collective-permute-start.5 = (bf16[4,128,512]{2,1,0:T(8,128)(2,1)S(1)}, bf16[4,128,512]{2,1,0:T(8,128)(2,1)S(1)}, u32[]{:S(2)}, u32[]{:S(2)}) collective-permute-start(bf16[4,128,512]{2,1,0:T(8,128)(2,1)S(1)} %collective-permute-done.4.refs_2_), channel_id=1, source_target_pairs={{0,4},{1,5},{2,6},{3,7},{4,8},{5,9},{6,10},{7,11},{8,12},{9,13},{1... | collective-permute-start | bytes 1572872 | tf_op jit(solution)/shard_map/ppermute | solution.py:40
  61.3 5.1 %collective-permute-start.9 = (bf16[4,128,512]{2,1,0:T(8,128)(2,1)}, bf16[4,128,512]{2,1,0:T(8,128)(2,1)S(1)}, u32[]{:S(2)}, u32[]{:S(2)}) collective-permute-start(bf16[4,128,512]{2,1,0:T(8,128)(2,1)} %collective-permute-done.8.refs_7_), channel_id=1, source_target_pairs={{0,28},{1,29},{2,30},{3,31},{4,0},{5,1},{6,2},{7,3},{8,4},{9,5},{1... | collective-permute-start | bytes 1572872 | tf_op jit(solution)/shard_map/ppermute | solution.py:40
  67.1 7.6 %collective-permute-done.5.refs_3_ = bf16[4,128,512]{2,1,0:T(8,128)(2,1)S(1)} collective-permute-done((bf16[4,128,512]{2,1,0:T(8,128)(2,1)S(1)}, bf16[4,128,512]{2,1,0:T(8,128)(2,1)S(1)}, u32[]{:S(2)}, u32[]{:S(2)}) %collective-permute-start.5) | collective-permute-done | bytes 524320 | tf_op jit(solution)/shard_map/ppermute | solution.py:40
  74.7 1.9 %collective-permute-start.6 = (bf16[2,128,512]{2,1,0:T(8,128)(2,1)S(1)}, bf16[2,128,512]{2,1,0:T(8,128)(2,1)S(1)}, u32[]{:S(2)}, u32[]{:S(2)}) collective-permute-start(bf16[2,128,512]{2,1,0:T(8,128)(2,1)S(1)} %slice.8), channel_id=1, source_target_pairs={{0,4},{1,5},{2,6},{3,7},{4,8},{5,9},{6,10},{7,11},{8,12},{9,13},{1... | collective-permute-start | bytes 786440 | tf_op jit(solution)/shard_map/ppermute | solution.py:40
  76.7 5.1 %collective-permute-start.10 = (bf16[2,128,512]{2,1,0:T(8,128)(2,1)S(1)}, bf16[2,128,512]{2,1,0:T(8,128)(2,1)S(1)}, u32[]{:S(2)}, u32[]{:S(2)}) collective-permute-start(bf16[2,128,512]{2,1,0:T(8,128)(2,1)S(1)} %slice.9), channel_id=1, source_target_pairs={{0,28},{1,29},{2,30},{3,31},{4,0},{5,1},{6,2},{7,3},{8,4},{9,5},{1... | collective-permute-start | bytes 786440 | tf_op jit(solution)/shard_map/ppermute | solution.py:40
  83.2 1.0 collective-permute-done.6.refs_4_
  84.2 1.5 %collective-permute-done.10.refs_5_ = bf16[2,128,512]{2,1,0:T(8,128)(2,1)S(1)} collective-permute-done((bf16[2,128,512]{2,1,0:T(8,128)(2,1)S(1)}, bf16[2,128,512]{2,1,0:T(8,128)(2,1)S(1)}, u32[]{:S(2)}, u32[]{:S(2)}) %collective-permute-start.10) | collective-permute-done | bytes 262176 | tf_op jit(solution)/shard_map/ppermute | solution.py:40
  85.7 2.3 %copy-done = bf16[1,1,128,128,128]{4,3,2,1,0:T(8,128)(2,1)S(1)} copy-done((bf16[1,1,128,128,128]{4,3,2,1,0:T(8,128)(2,1)S(1)}, bf16[1,1,128,128,128]{4,3,2,1,0:T(8,128)(2,1)}, u32[]{:S(2)}) %copy-start) | copy-done | bytes 4194328
  88.0 3.8 %shard_map.64 = (f32[8,128,256]{2,1,0:T(8,128)S(1)}, bf16[8,128,256]{2,1,0:T(8,128)(2,1)S(1)}) custom-call(s32[258]{0:T(512)S(1)} %pad_add_fusion.meta, bf16[128,128,128]{2,1,0:T(8,128)(2,1)S(1)} %bitcast.14, bf16[4,128,512]{2,1,0:T(8,128)(2,1)S(1)} %pad_maximum_fusion.refs_0_, bf16[4,128,512]{2,1,0:T(8,128)(2,1)S(1)} %collective-permute-done.3.refs_1_, ...), custom_call_target="tpu_custom_call" | custom-call | flops 1073741824 | bytes 8388608 | tf_op jit(solution)/shard_map/pallas_call | solution.py:93
  91.8 1.9 %collective-permute-start.11 = (bf16[8,128,256]{2,1,0:T(8,128)(2,1)S(1)}, bf16[8,128,256]{2,1,0:T(8,128)(2,1)S(1)}, u32[]{:S(2)}, u32[]{:S(2)}) collective-permute-start(bf16[8,128,256]{2,1,0:T(8,128)(2,1)S(1)} %get-tuple-element.10), channel_id=1, source_target_pairs={{0,32},{1,33},{2,34},{3,35},{4,36},{5,37},{6,38},{7,39},{8,40},{9,... | collective-permute-start | bytes 1572872 | tf_op jit(solution)/shard_map/ppermute | solution.py:40
  93.7 1.9 %collective-permute-done.11.came = bf16[8,128,256]{2,1,0:T(8,128)(2,1)S(1)} collective-permute-done((bf16[8,128,256]{2,1,0:T(8,128)(2,1)S(1)}, bf16[8,128,256]{2,1,0:T(8,128)(2,1)S(1)}, u32[]{:S(2)}, u32[]{:S(2)}) %collective-permute-start.11) | collective-permute-done | bytes 524320 | tf_op jit(solution)/shard_map/ppermute | solution.py:40
  95.7 0.8 copy-done.2
  96.5 10.1 %all-to-all-start = ((bf16[8,128,256]{2,1,0:T(8,128)(2,1)}), bf16[8,128,256]{2,1,0:T(8,128)(2,1)}, u32[]{:S(2)}, u32[]{:S(2)}) async-start(bf16[8,128,256]{2,1,0:T(8,128)(2,1)} %copy-done.2), calls=%async_computation | async-start | bytes 1048576 | tf_op jit(solution)/shard_map/all_to_all | solution.py:174
  106.6 2.2 %copy-done.1 = bf16[1,1,128,128,128]{4,3,2,1,0:T(8,128)(2,1)S(1)} copy-done((bf16[1,1,128,128,128]{4,3,2,1,0:T(8,128)(2,1)S(1)}, bf16[1,1,128,128,128]{4,3,2,1,0:T(8,128)(2,1)}, u32[]{:S(2)}) %copy-start.1) | copy-done | bytes 4194328
  108.8 0.9 copy-done.4
  109.7 3.8 %shard_map.66 = (f32[8,128,256]{2,1,0:T(8,128)S(1)}, bf16[8,128,256]{2,1,0:T(8,128)(2,1)S(1)}) custom-call(s32[258]{0:T(512)S(1)} %pad_add_fusion.meta, bf16[128,128,128]{2,1,0:T(8,128)(2,1)S(1)} %bitcast.15, bf16[4,128,512]{2,1,0:T(8,128)(2,1)S(1)} %pad_maximum_fusion.refs_0_, bf16[4,128,512]{2,1,0:T(8,128)(2,1)S(1)} %collective-permute-done.3.refs_1_, ...), custom_call_target="tpu_custom_call" | custom-call | flops 1073741824 | bytes 8388608 | tf_op jit(solution)/shard_map/pallas_call | solution.py:93
  113.6 1.9 %collective-permute-start.12 = (bf16[8,128,256]{2,1,0:T(8,128)(2,1)S(1)}, bf16[8,128,256]{2,1,0:T(8,128)(2,1)S(1)}, u32[]{:S(2)}, u32[]{:S(2)}) collective-permute-start(bf16[8,128,256]{2,1,0:T(8,128)(2,1)S(1)} %get-tuple-element.12), channel_id=1, source_target_pairs={{0,32},{1,33},{2,34},{3,35},{4,36},{5,37},{6,38},{7,39},{8,40},{9,... | collective-permute-start | bytes 1572872 | tf_op jit(solution)/shard_map/ppermute | solution.py:40
  115.5 1.9 %collective-permute-done.12.came = bf16[8,128,256]{2,1,0:T(8,128)(2,1)S(1)} collective-permute-done((bf16[8,128,256]{2,1,0:T(8,128)(2,1)S(1)}, bf16[8,128,256]{2,1,0:T(8,128)(2,1)S(1)}, u32[]{:S(2)}, u32[]{:S(2)}) %collective-permute-start.12) | collective-permute-done | bytes 524320 | tf_op jit(solution)/shard_map/ppermute | solution.py:40
  117.5 17.7 %all_to_all.10.refs_1_ = bf16[8,128,256]{2,1,0:T(8,128)(2,1)S(1)} all-to-all(bf16[8,128,256]{2,1,0:T(8,128)(2,1)S(1)} %shard_map.67), channel_id=1, replica_groups={{0,64,128,192,256,320,384,448},{32,96,160,224,288,352,416,480},{1,65,12..., dimensions={0} | all-to-all | bytes 1048576 | tf_op jit(solution)/shard_map/all_to_all | solution.py:174
  135.2 1.9 %shard_map.68 = bf16[128,512]{1,0:T(8,128)(2,1)} custom-call(bf16[128,512]{1,0:T(8,128)(2,1)S(1)} %bitcast.16, bf16[8,128,256]{2,1,0:T(8,128)(2,1)} %all-to-all-done.refs_0_, bf16[8,128,256]{2,1,0:T(8,128)(2,1)S(1)} %all_to_all.10.refs_1_), custom_call_target="tpu_custom_call" | custom-call | flops 589824 | bytes 1310720 | tf_op jit(solution)/shard_map/pallas_call | solution.py:147
  (19 shorter events, 1.6 us)
Async XLA Ops:
  0.0 15.0 %collective-permute-start.2 = (bf16[128,512]{1,0:T(8,128)(2,1)}, bf16[128,512]{1,0:T(8,128)(2,1)S(1)}, u32[]{:S(2)}, u32[]{:S(2)}) collective-permute-start(bf16[128,512]{1,0:T(8,128)(2,1)} %bitcast.17), channel_id=1, source_target_pairs={{0,3},{1,0},{2,1},{3,2},{4,7},{5,4},{6,5},{7,6},{8,11},{9,8},{10,9... | collective-permute-start | bytes 393224 | tf_op jit(solution)/shard_map/ppermute | solution.py:40
  7.6 12.6 %collective-permute-start.1 = (bf16[128,512]{1,0:T(8,128)(2,1)}, bf16[128,512]{1,0:T(8,128)(2,1)S(1)}, u32[]{:S(2)}, u32[]{:S(2)}) collective-permute-start(bf16[128,512]{1,0:T(8,128)(2,1)} %bitcast.18), channel_id=1, source_target_pairs={{0,2},{1,3},{2,0},{3,1},{4,6},{5,7},{6,4},{7,5},{8,10},{9,11},{10,... | collective-permute-start | bytes 393224 | tf_op jit(solution)/shard_map/ppermute | solution.py:40
  10.0 11.2 %collective-permute-start = (bf16[128,512]{1,0:T(8,128)(2,1)}, bf16[128,512]{1,0:T(8,128)(2,1)S(1)}, u32[]{:S(2)}, u32[]{:S(2)}) collective-permute-start(bf16[128,512]{1,0:T(8,128)(2,1)} %bitcast.19), channel_id=1, source_target_pairs={{0,1},{1,2},{2,3},{3,0},{4,5},{5,6},{6,7},{7,4},{8,9},{9,10},{10,1... | collective-permute-start | bytes 393224 | tf_op jit(solution)/shard_map/ppermute | solution.py:40
  22.2 21.0 %collective-permute-start.3 = (bf16[4,128,512]{2,1,0:T(8,128)(2,1)S(1)}, bf16[4,128,512]{2,1,0:T(8,128)(2,1)S(1)}, u32[]{:S(2)}, u32[]{:S(2)}) collective-permute-start(bf16[4,128,512]{2,1,0:T(8,128)(2,1)S(1)} %pad_maximum_fusion.refs_0_), channel_id=1, source_target_pairs={{0,4},{1,5},{2,6},{3,7},{4,8},{5,9},{6,10},{7,11},{8,12},{9,13},{1... | collective-permute-start | bytes 1572872 | tf_op jit(solution)/shard_map/ppermute | solution.py:40
  24.6 20.5 %collective-permute-start.7 = (bf16[4,128,512]{2,1,0:T(8,128)(2,1)S(1)}, bf16[4,128,512]{2,1,0:T(8,128)(2,1)S(1)}, u32[]{:S(2)}, u32[]{:S(2)}) collective-permute-start(bf16[4,128,512]{2,1,0:T(8,128)(2,1)S(1)} %pad_maximum_fusion.refs_0_), channel_id=1, source_target_pairs={{0,28},{1,29},{2,30},{3,31},{4,0},{5,1},{6,2},{7,3},{8,4},{9,5},{1... | collective-permute-start | bytes 1572872 | tf_op jit(solution)/shard_map/ppermute | solution.py:40
  43.2 16.2 %collective-permute-start.4 = (bf16[4,128,512]{2,1,0:T(8,128)(2,1)S(1)}, bf16[4,128,512]{2,1,0:T(8,128)(2,1)S(1)}, u32[]{:S(2)}, u32[]{:S(2)}) collective-permute-start(bf16[4,128,512]{2,1,0:T(8,128)(2,1)S(1)} %collective-permute-done.3.refs_1_), channel_id=1, source_target_pairs={{0,4},{1,5},{2,6},{3,7},{4,8},{5,9},{6,10},{7,11},{8,12},{9,13},{1... | collective-permute-start | bytes 1572872 | tf_op jit(solution)/shard_map/ppermute | solution.py:40
  45.1 16.2 %collective-permute-start.8 = (bf16[4,128,512]{2,1,0:T(8,128)(2,1)S(1)}, bf16[4,128,512]{2,1,0:T(8,128)(2,1)}, u32[]{:S(2)}, u32[]{:S(2)}) collective-permute-start(bf16[4,128,512]{2,1,0:T(8,128)(2,1)S(1)} %collective-permute-done.7.refs_8_), channel_id=1, source_target_pairs={{0,28},{1,29},{2,30},{3,31},{4,0},{5,1},{6,2},{7,3},{8,4},{9,5},{1... | collective-permute-start | bytes 1572872 | tf_op jit(solution)/shard_map/ppermute | solution.py:40
  59.4 15.3 %collective-permute-start.5 = (bf16[4,128,512]{2,1,0:T(8,128)(2,1)S(1)}, bf16[4,128,512]{2,1,0:T(8,128)(2,1)S(1)}, u32[]{:S(2)}, u32[]{:S(2)}) collective-permute-start(bf16[4,128,512]{2,1,0:T(8,128)(2,1)S(1)} %collective-permute-done.4.refs_2_), channel_id=1, source_target_pairs={{0,4},{1,5},{2,6},{3,7},{4,8},{5,9},{6,10},{7,11},{8,12},{9,13},{1... | collective-permute-start | bytes 1572872 | tf_op jit(solution)/shard_map/ppermute | solution.py:40
  61.3 15.3 %collective-permute-start.9 = (bf16[4,128,512]{2,1,0:T(8,128)(2,1)}, bf16[4,128,512]{2,1,0:T(8,128)(2,1)S(1)}, u32[]{:S(2)}, u32[]{:S(2)}) collective-permute-start(bf16[4,128,512]{2,1,0:T(8,128)(2,1)} %collective-permute-done.8.refs_7_), channel_id=1, source_target_pairs={{0,28},{1,29},{2,30},{3,31},{4,0},{5,1},{6,2},{7,3},{8,4},{9,5},{1... | collective-permute-start | bytes 1572872 | tf_op jit(solution)/shard_map/ppermute | solution.py:40
  74.7 9.5 %collective-permute-start.6 = (bf16[2,128,512]{2,1,0:T(8,128)(2,1)S(1)}, bf16[2,128,512]{2,1,0:T(8,128)(2,1)S(1)}, u32[]{:S(2)}, u32[]{:S(2)}) collective-permute-start(bf16[2,128,512]{2,1,0:T(8,128)(2,1)S(1)} %slice.8), channel_id=1, source_target_pairs={{0,4},{1,5},{2,6},{3,7},{4,8},{5,9},{6,10},{7,11},{8,12},{9,13},{1... | collective-permute-start | bytes 786440 | tf_op jit(solution)/shard_map/ppermute | solution.py:40
  76.7 9.0 %collective-permute-start.10 = (bf16[2,128,512]{2,1,0:T(8,128)(2,1)S(1)}, bf16[2,128,512]{2,1,0:T(8,128)(2,1)S(1)}, u32[]{:S(2)}, u32[]{:S(2)}) collective-permute-start(bf16[2,128,512]{2,1,0:T(8,128)(2,1)S(1)} %slice.9), channel_id=1, source_target_pairs={{0,28},{1,29},{2,30},{3,31},{4,0},{5,1},{6,2},{7,3},{8,4},{9,5},{1... | collective-permute-start | bytes 786440 | tf_op jit(solution)/shard_map/ppermute | solution.py:40
  85.7 6.1 %copy-start.3 = (bf16[2,128,512]{2,1,0:T(8,128)(2,1)}, bf16[2,128,512]{2,1,0:T(8,128)(2,1)S(1)}, u32[]{:S(2)}) copy-start(bf16[2,128,512]{2,1,0:T(8,128)(2,1)S(1)} %collective-permute-done.10.refs_5_) | copy-start | bytes 786436
  85.7 2.3 %copy-start = (bf16[1,1,128,128,128]{4,3,2,1,0:T(8,128)(2,1)S(1)}, bf16[1,1,128,128,128]{4,3,2,1,0:T(8,128)(2,1)}, u32[]{:S(2)}) copy-start(bf16[1,1,128,128,128]{4,3,2,1,0:T(8,128)(2,1)} %param.7) | copy-start | bytes 12582916
  91.8 3.8 %collective-permute-start.11 = (bf16[8,128,256]{2,1,0:T(8,128)(2,1)S(1)}, bf16[8,128,256]{2,1,0:T(8,128)(2,1)S(1)}, u32[]{:S(2)}, u32[]{:S(2)}) collective-permute-start(bf16[8,128,256]{2,1,0:T(8,128)(2,1)S(1)} %get-tuple-element.10), channel_id=1, source_target_pairs={{0,32},{1,33},{2,34},{3,35},{4,36},{5,37},{6,38},{7,39},{8,40},{9,... | collective-permute-start | bytes 1572872 | tf_op jit(solution)/shard_map/ppermute | solution.py:40
  95.7 0.8 copy-start.2
  96.5 21.0 %all-to-all-start = ((bf16[8,128,256]{2,1,0:T(8,128)(2,1)}), bf16[8,128,256]{2,1,0:T(8,128)(2,1)}, u32[]{:S(2)}, u32[]{:S(2)}) async-start(bf16[8,128,256]{2,1,0:T(8,128)(2,1)} %copy-done.2), calls=%async_computation | async-start | bytes 1048576 | tf_op jit(solution)/shard_map/all_to_all | solution.py:174
  106.6 2.2 %copy-start.1 = (bf16[1,1,128,128,128]{4,3,2,1,0:T(8,128)(2,1)S(1)}, bf16[1,1,128,128,128]{4,3,2,1,0:T(8,128)(2,1)}, u32[]{:S(2)}) copy-start(bf16[1,1,128,128,128]{4,3,2,1,0:T(8,128)(2,1)} %param.7) | copy-start | bytes 12582916
  108.8 0.9 copy-start.4
  109.7 25.5 %copy-start.5 = (bf16[1,1,128,512]{3,2,1,0:T(8,128)(2,1)S(1)}, bf16[1,1,128,512]{3,2,1,0:T(8,128)(2,1)}, u32[]{:S(2)}) copy-start(bf16[1,1,128,512]{3,2,1,0:T(8,128)(2,1)} %param.11) | copy-start | bytes 393220
  113.6 3.8 %collective-permute-start.12 = (bf16[8,128,256]{2,1,0:T(8,128)(2,1)S(1)}, bf16[8,128,256]{2,1,0:T(8,128)(2,1)S(1)}, u32[]{:S(2)}, u32[]{:S(2)}) collective-permute-start(bf16[8,128,256]{2,1,0:T(8,128)(2,1)S(1)} %get-tuple-element.12), channel_id=1, source_target_pairs={{0,32},{1,33},{2,34},{3,35},{4,36},{5,37},{6,38},{7,39},{8,40},{9,... | collective-permute-start | bytes 1572872 | tf_op jit(solution)/shard_map/ppermute | solution.py:40

commit v2 on v1

--- a/solution.py
+++ b/solution.py
@@ -11,7 +11,7 @@
 YL, X, CORE, Z, YH = 2, 4, 2, 8, 4
 AXES = ("row", "col")
 GROUP = 16
-PARTS = 2
+PARTS = 1
 
 
 def place(yl, x, core, z, yh):

time: 138 us -> 129 us (0.935)
  the two profiles are of different devices: /device:TPU:16 before, /device:TPU:32 now
where the time goes in v2:
time: 129 us; the launch traced here: 128 us
  starting transfers between devices  51.6 us (40%)
  waiting for transfers between devices  41.4 us (32%)
  blocking collectives  20.8 us (16%)
  Pallas kernels  9.01 us (7%)
  other arithmetic  2.37 us (2%)
  local copies, waits for them, and re-layouts  2.23 us (2%)
    ppermute x12, starting transfers between devices, send(): return lax.ppermute(value, AXES, moves(step))  51.6 us
    ppermute x12, waiting for transfers between devices, send(): return lax.ppermute(value, AXES, moves(step))  41.4 us
    all_to_all x1, blocking collectives, reduce_part(): lax.all_to_all(both, 'row', 0, 0, axis_index_groups=groups, tiled=True)  20.8 us
    pallas_call x1, Pallas kernels, spmm(): pl.pallas_call(functools.partial(spmm_kernel, first), out_shape=(jax.Shap...  7.99 us
  transfers between devices with their start and end apart: 12, of which 8 were waited for; matrix products, arithmetic and copies ran while one was open for 1% of the time, Pallas kernels for 0%

profile of v2, /device:TPU:32, one launch (start us, length us, event | category | flops | bytes accessed | tf_op | source)
XLA Modules:
  0.0 128.3 jit_solution(16324006827197773018)
XLA Ops:
  0.0 2.2 %collective-permute-start.2 = (bf16[128,512]{1,0:T(8,128)(2,1)}, bf16[128,512]{1,0:T(8,128)(2,1)S(1)}, u32[]{:S(2)}, u32[]{:S(2)}) collective-permute-start(bf16[128,512]{1,0:T(8,128)(2,1)} %bitcast.16), channel_id=1, source_target_pairs={{0,3},{1,0},{2,1},{3,2},{4,7},{5,4},{6,5},{7,6},{8,11},{9,8},{10,9... | collective-permute-start | bytes 393224 | tf_op jit(solution)/shard_map/ppermute | solution.py:40
  2.2 7.1 %collective-permute-start.1 = (bf16[128,512]{1,0:T(8,128)(2,1)}, bf16[128,512]{1,0:T(8,128)(2,1)S(1)}, u32[]{:S(2)}, u32[]{:S(2)}) collective-permute-start(bf16[128,512]{1,0:T(8,128)(2,1)} %bitcast.17), channel_id=1, source_target_pairs={{0,2},{1,3},{2,0},{3,1},{4,6},{5,7},{6,4},{7,5},{8,10},{9,11},{10,... | collective-permute-start | bytes 393224 | tf_op jit(solution)/shard_map/ppermute | solution.py:40
  9.3 4.8 %collective-permute-start = (bf16[128,512]{1,0:T(8,128)(2,1)}, bf16[128,512]{1,0:T(8,128)(2,1)S(1)}, u32[]{:S(2)}, u32[]{:S(2)}) collective-permute-start(bf16[128,512]{1,0:T(8,128)(2,1)} %bitcast.18), channel_id=1, source_target_pairs={{0,1},{1,2},{2,3},{3,0},{4,5},{5,6},{6,7},{7,4},{8,9},{9,10},{10,1... | collective-permute-start | bytes 393224 | tf_op jit(solution)/shard_map/ppermute | solution.py:40
  14.1 0.0 collective-permute-done.2
  14.2 0.6 collective-permute-done.1
  14.8 7.1 %collective-permute-done = bf16[128,512]{1,0:T(8,128)(2,1)S(1)} collective-permute-done((bf16[128,512]{1,0:T(8,128)(2,1)}, bf16[128,512]{1,0:T(8,128)(2,1)S(1)}, u32[]{:S(2)}, u32[]{:S(2)}) %collective-permute-start) | collective-permute-done | bytes 131104 | tf_op jit(solution)/shard_map/ppermute | solution.py:40
  21.8 1.0 pad_maximum_fusion.refs_0_
  22.8 10.9 %collective-permute-start.7 = (bf16[4,128,512]{2,1,0:T(8,128)(2,1)S(1)}, bf16[4,128,512]{2,1,0:T(8,128)(2,1)S(1)}, u32[]{:S(2)}, u32[]{:S(2)}) collective-permute-start(bf16[4,128,512]{2,1,0:T(8,128)(2,1)S(1)} %pad_maximum_fusion.refs_0_), channel_id=1, source_target_pairs={{0,28},{1,29},{2,30},{3,31},{4,0},{5,1},{6,2},{7,3},{8,4},{9,5},{1... | collective-permute-start | bytes 1572872 | tf_op jit(solution)/shard_map/ppermute | solution.py:40
  33.8 1.9 %collective-permute-start.3 = (bf16[4,128,512]{2,1,0:T(8,128)(2,1)S(1)}, bf16[4,128,512]{2,1,0:T(8,128)(2,1)S(1)}, u32[]{:S(2)}, u32[]{:S(2)}) collective-permute-start(bf16[4,128,512]{2,1,0:T(8,128)(2,1)S(1)} %pad_maximum_fusion.refs_0_), channel_id=1, source_target_pairs={{0,4},{1,5},{2,6},{3,7},{4,8},{5,9},{6,10},{7,11},{8,12},{9,13},{1... | collective-permute-start | bytes 1572872 | tf_op jit(solution)/shard_map/ppermute | solution.py:40
  35.7 9.4 %collective-permute-done.7.refs_8_ = bf16[4,128,512]{2,1,0:T(8,128)(2,1)S(1)} collective-permute-done((bf16[4,128,512]{2,1,0:T(8,128)(2,1)S(1)}, bf16[4,128,512]{2,1,0:T(8,128)(2,1)S(1)}, u32[]{:S(2)}, u32[]{:S(2)}) %collective-permute-start.7) | collective-permute-done | bytes 524320 | tf_op jit(solution)/shard_map/ppermute | solution.py:40
  45.1 5.6 %collective-permute-start.8 = (bf16[4,128,512]{2,1,0:T(8,128)(2,1)S(1)}, bf16[4,128,512]{2,1,0:T(8,128)(2,1)S(1)}, u32[]{:S(2)}, u32[]{:S(2)}) collective-permute-start(bf16[4,128,512]{2,1,0:T(8,128)(2,1)S(1)} %collective-permute-done.7.refs_8_), channel_id=1, source_target_pairs={{0,28},{1,29},{2,30},{3,31},{4,0},{5,1},{6,2},{7,3},{8,4},{9,5},{1... | collective-permute-start | bytes 1572872 | tf_op jit(solution)/shard_map/ppermute | solution.py:40
  50.7 0.0 collective-permute-done.3.refs_1_
  50.7 1.9 %collective-permute-start.4 = (bf16[4,128,512]{2,1,0:T(8,128)(2,1)S(1)}, bf16[4,128,512]{2,1,0:T(8,128)(2,1)}, u32[]{:S(2)}, u32[]{:S(2)}) collective-permute-start(bf16[4,128,512]{2,1,0:T(8,128)(2,1)S(1)} %collective-permute-done.3.refs_1_), channel_id=1, source_target_pairs={{0,4},{1,5},{2,6},{3,7},{4,8},{5,9},{6,10},{7,11},{8,12},{9,13},{1... | collective-permute-start | bytes 1572872 | tf_op jit(solution)/shard_map/ppermute | solution.py:40
  52.7 8.6 %collective-permute-done.8.refs_7_ = bf16[4,128,512]{2,1,0:T(8,128)(2,1)S(1)} collective-permute-done((bf16[4,128,512]{2,1,0:T(8,128)(2,1)S(1)}, bf16[4,128,512]{2,1,0:T(8,128)(2,1)S(1)}, u32[]{:S(2)}, u32[]{:S(2)}) %collective-permute-start.8) | collective-permute-done | bytes 524320 | tf_op jit(solution)/shard_map/ppermute | solution.py:40
  61.2 5.6 %collective-permute-start.9 = (bf16[4,128,512]{2,1,0:T(8,128)(2,1)S(1)}, bf16[4,128,512]{2,1,0:T(8,128)(2,1)S(1)}, u32[]{:S(2)}, u32[]{:S(2)}) collective-permute-start(bf16[4,128,512]{2,1,0:T(8,128)(2,1)S(1)} %collective-permute-done.8.refs_7_), channel_id=1, source_target_pairs={{0,28},{1,29},{2,30},{3,31},{4,0},{5,1},{6,2},{7,3},{8,4},{9,5},{1... | collective-permute-start | bytes 1572872 | tf_op jit(solution)/shard_map/ppermute | solution.py:40
  66.8 1.9 %collective-permute-start.5 = (bf16[4,128,512]{2,1,0:T(8,128)(2,1)}, bf16[4,128,512]{2,1,0:T(8,128)(2,1)S(1)}, u32[]{:S(2)}, u32[]{:S(2)}) collective-permute-start(bf16[4,128,512]{2,1,0:T(8,128)(2,1)} %collective-permute-done.4.refs_2_), channel_id=1, source_target_pairs={{0,4},{1,5},{2,6},{3,7},{4,8},{5,9},{6,10},{7,11},{8,12},{9,13},{1... | collective-permute-start | bytes 1572872 | tf_op jit(solution)/shard_map/ppermute | solution.py:40
  69.4 7.0 %collective-permute-done.9.refs_6_ = bf16[4,128,512]{2,1,0:T(8,128)(2,1)S(1)} collective-permute-done((bf16[4,128,512]{2,1,0:T(8,128)(2,1)S(1)}, bf16[4,128,512]{2,1,0:T(8,128)(2,1)S(1)}, u32[]{:S(2)}, u32[]{:S(2)}) %collective-permute-start.9) | collective-permute-done | bytes 524320 | tf_op jit(solution)/shard_map/ppermute | solution.py:40
  76.4 5.6 %collective-permute-start.10 = (bf16[2,128,512]{2,1,0:T(8,128)(2,1)S(1)}, bf16[2,128,512]{2,1,0:T(8,128)(2,1)S(1)}, u32[]{:S(2)}, u32[]{:S(2)}) collective-permute-start(bf16[2,128,512]{2,1,0:T(8,128)(2,1)S(1)} %slice.9), channel_id=1, source_target_pairs={{0,28},{1,29},{2,30},{3,31},{4,0},{5,1},{6,2},{7,3},{8,4},{9,5},{1... | collective-permute-start | bytes 786440 | tf_op jit(solution)/shard_map/ppermute | solution.py:40
  82.0 0.0 collective-permute-done.5.refs_3_
  82.1 1.9 %collective-permute-start.6 = (bf16[2,128,512]{2,1,0:T(8,128)(2,1)S(1)}, bf16[2,128,512]{2,1,0:T(8,128)(2,1)S(1)}, u32[]{:S(2)}, u32[]{:S(2)}) collective-permute-start(bf16[2,128,512]{2,1,0:T(8,128)(2,1)S(1)} %slice.8), channel_id=1, source_target_pairs={{0,4},{1,5},{2,6},{3,7},{4,8},{5,9},{6,10},{7,11},{8,12},{9,13},{1... | collective-permute-start | bytes 786440 | tf_op jit(solution)/shard_map/ppermute | solution.py:40
  84.0 0.7 add_bitcast_fusion
  84.7 0.7 pad_add_fusion.meta
  85.4 0.5 collective-permute-done.10.refs_5_
  85.9 5.6 %collective-permute-done.6.refs_4_ = bf16[2,128,512]{2,1,0:T(8,128)(2,1)S(1)} collective-permute-done((bf16[2,128,512]{2,1,0:T(8,128)(2,1)S(1)}, bf16[2,128,512]{2,1,0:T(8,128)(2,1)S(1)}, u32[]{:S(2)}, u32[]{:S(2)}) %collective-permute-start.6) | collective-permute-done | bytes 262176 | tf_op jit(solution)/shard_map/ppermute | solution.py:40
  91.5 2.2 %copy-done = bf16[1,1,128,128,128]{4,3,2,1,0:T(8,128)(2,1)S(1)} copy-done((bf16[1,1,128,128,128]{4,3,2,1,0:T(8,128)(2,1)S(1)}, bf16[1,1,128,128,128]{4,3,2,1,0:T(8,128)(2,1)}, u32[]{:S(2)}) %copy-start) | copy-done | bytes 4194328
  93.7 8.0 %shard_map.64 = (f32[8,128,512]{2,1,0:T(8,128)S(1)}, bf16[8,128,512]{2,1,0:T(8,128)(2,1)S(1)}) custom-call(s32[258]{0:T(512)S(1)} %pad_add_fusion.meta, bf16[128,128,128]{2,1,0:T(8,128)(2,1)S(1)} %bitcast.14, bf16[4,128,512]{2,1,0:T(8,128)(2,1)S(1)} %pad_maximum_fusion.refs_0_, bf16[4,128,512]{2,1,0:T(8,128)(2,1)S(1)} %collective-permute-done.3.refs_1_, ...), custom_call_target="tpu_custom_call" | custom-call | flops 2147483648 | bytes 8388608 | tf_op jit(solution)/shard_map/pallas_call | solution.py:93
  101.7 0.0 copy-start.1
  101.7 2.1 %collective-permute-start.11 = (bf16[8,128,512]{2,1,0:T(8,128)(2,1)S(1)}, bf16[8,128,512]{2,1,0:T(8,128)(2,1)S(1)}, u32[]{:S(2)}, u32[]{:S(2)}) collective-permute-start(bf16[8,128,512]{2,1,0:T(8,128)(2,1)S(1)} %get-tuple-element.8), channel_id=1, source_target_pairs={{0,32},{1,33},{2,34},{3,35},{4,36},{5,37},{6,38},{7,39},{8,40},{9,... | collective-permute-start | bytes 3145736 | tf_op jit(solution)/shard_map/ppermute | solution.py:40
  103.8 2.6 %collective-permute-done.11.came = bf16[8,128,512]{2,1,0:T(8,128)(2,1)S(1)} collective-permute-done((bf16[8,128,512]{2,1,0:T(8,128)(2,1)S(1)}, bf16[8,128,512]{2,1,0:T(8,128)(2,1)S(1)}, u32[]{:S(2)}, u32[]{:S(2)}) %collective-permute-start.11) | collective-permute-done | bytes 1048608 | tf_op jit(solution)/shard_map/ppermute | solution.py:40
  106.4 0.2 shard_map.65
  106.6 20.8 %all_to_all.5.refs_0_ = bf16[8,128,512]{2,1,0:T(8,128)(2,1)S(1)} all-to-all(bf16[8,128,512]{2,1,0:T(8,128)(2,1)S(1)} %shard_map.65), channel_id=1, replica_groups={{0,64,128,192,256,320,384,448},{32,96,160,224,288,352,416,480},{1,65,12..., dimensions={0} | all-to-all | bytes 2097152 | tf_op jit(solution)/shard_map/all_to_all | solution.py:174
  127.5 0.8 shard_map.66
  (5 shorter events, 0.0 us)
Async XLA Ops:
  0.0 14.1 %collective-permute-start.2 = (bf16[128,512]{1,0:T(8,128)(2,1)}, bf16[128,512]{1,0:T(8,128)(2,1)S(1)}, u32[]{:S(2)}, u32[]{:S(2)}) collective-permute-start(bf16[128,512]{1,0:T(8,128)(2,1)} %bitcast.16), channel_id=1, source_target_pairs={{0,3},{1,0},{2,1},{3,2},{4,7},{5,4},{6,5},{7,6},{8,11},{9,8},{10,9... | collective-permute-start | bytes 393224 | tf_op jit(solution)/shard_map/ppermute | solution.py:40
  2.2 12.5 %collective-permute-start.1 = (bf16[128,512]{1,0:T(8,128)(2,1)}, bf16[128,512]{1,0:T(8,128)(2,1)S(1)}, u32[]{:S(2)}, u32[]{:S(2)}) collective-permute-start(bf16[128,512]{1,0:T(8,128)(2,1)} %bitcast.17), channel_id=1, source_target_pairs={{0,2},{1,3},{2,0},{3,1},{4,6},{5,7},{6,4},{7,5},{8,10},{9,11},{10,... | collective-permute-start | bytes 393224 | tf_op jit(solution)/shard_map/ppermute | solution.py:40
  9.3 12.5 %collective-permute-start = (bf16[128,512]{1,0:T(8,128)(2,1)}, bf16[128,512]{1,0:T(8,128)(2,1)S(1)}, u32[]{:S(2)}, u32[]{:S(2)}) collective-permute-start(bf16[128,512]{1,0:T(8,128)(2,1)} %bitcast.18), channel_id=1, source_target_pairs={{0,1},{1,2},{2,3},{3,0},{4,5},{5,6},{6,7},{7,4},{8,9},{9,10},{10,1... | collective-permute-start | bytes 393224 | tf_op jit(solution)/shard_map/ppermute | solution.py:40
  22.8 22.3 %collective-permute-start.7 = (bf16[4,128,512]{2,1,0:T(8,128)(2,1)S(1)}, bf16[4,128,512]{2,1,0:T(8,128)(2,1)S(1)}, u32[]{:S(2)}, u32[]{:S(2)}) collective-permute-start(bf16[4,128,512]{2,1,0:T(8,128)(2,1)S(1)} %pad_maximum_fusion.refs_0_), channel_id=1, source_target_pairs={{0,28},{1,29},{2,30},{3,31},{4,0},{5,1},{6,2},{7,3},{8,4},{9,5},{1... | collective-permute-start | bytes 1572872 | tf_op jit(solution)/shard_map/ppermute | solution.py:40
  33.8 16.9 %collective-permute-start.3 = (bf16[4,128,512]{2,1,0:T(8,128)(2,1)S(1)}, bf16[4,128,512]{2,1,0:T(8,128)(2,1)S(1)}, u32[]{:S(2)}, u32[]{:S(2)}) collective-permute-start(bf16[4,128,512]{2,1,0:T(8,128)(2,1)S(1)} %pad_maximum_fusion.refs_0_), channel_id=1, source_target_pairs={{0,4},{1,5},{2,6},{3,7},{4,8},{5,9},{6,10},{7,11},{8,12},{9,13},{1... | collective-permute-start | bytes 1572872 | tf_op jit(solution)/shard_map/ppermute | solution.py:40
  45.1 16.1 %collective-permute-start.8 = (bf16[4,128,512]{2,1,0:T(8,128)(2,1)S(1)}, bf16[4,128,512]{2,1,0:T(8,128)(2,1)S(1)}, u32[]{:S(2)}, u32[]{:S(2)}) collective-permute-start(bf16[4,128,512]{2,1,0:T(8,128)(2,1)S(1)} %collective-permute-done.7.refs_8_), channel_id=1, source_target_pairs={{0,28},{1,29},{2,30},{3,31},{4,0},{5,1},{6,2},{7,3},{8,4},{9,5},{1... | collective-permute-start | bytes 1572872 | tf_op jit(solution)/shard_map/ppermute | solution.py:40
  50.7 16.1 %collective-permute-start.4 = (bf16[4,128,512]{2,1,0:T(8,128)(2,1)S(1)}, bf16[4,128,512]{2,1,0:T(8,128)(2,1)}, u32[]{:S(2)}, u32[]{:S(2)}) collective-permute-start(bf16[4,128,512]{2,1,0:T(8,128)(2,1)S(1)} %collective-permute-done.3.refs_1_), channel_id=1, source_target_pairs={{0,4},{1,5},{2,6},{3,7},{4,8},{5,9},{6,10},{7,11},{8,12},{9,13},{1... | collective-permute-start | bytes 1572872 | tf_op jit(solution)/shard_map/ppermute | solution.py:40
  61.2 15.2 %collective-permute-start.9 = (bf16[4,128,512]{2,1,0:T(8,128)(2,1)S(1)}, bf16[4,128,512]{2,1,0:T(8,128)(2,1)S(1)}, u32[]{:S(2)}, u32[]{:S(2)}) collective-permute-start(bf16[4,128,512]{2,1,0:T(8,128)(2,1)S(1)} %collective-permute-done.8.refs_7_), channel_id=1, source_target_pairs={{0,28},{1,29},{2,30},{3,31},{4,0},{5,1},{6,2},{7,3},{8,4},{9,5},{1... | collective-permute-start | bytes 1572872 | tf_op jit(solution)/shard_map/ppermute | solution.py:40
  66.8 15.2 %collective-permute-start.5 = (bf16[4,128,512]{2,1,0:T(8,128)(2,1)}, bf16[4,128,512]{2,1,0:T(8,128)(2,1)S(1)}, u32[]{:S(2)}, u32[]{:S(2)}) collective-permute-start(bf16[4,128,512]{2,1,0:T(8,128)(2,1)} %collective-permute-done.4.refs_2_), channel_id=1, source_target_pairs={{0,4},{1,5},{2,6},{3,7},{4,8},{5,9},{6,10},{7,11},{8,12},{9,13},{1... | collective-permute-start | bytes 1572872 | tf_op jit(solution)/shard_map/ppermute | solution.py:40
  76.4 9.5 %collective-permute-start.10 = (bf16[2,128,512]{2,1,0:T(8,128)(2,1)S(1)}, bf16[2,128,512]{2,1,0:T(8,128)(2,1)S(1)}, u32[]{:S(2)}, u32[]{:S(2)}) collective-permute-start(bf16[2,128,512]{2,1,0:T(8,128)(2,1)S(1)} %slice.9), channel_id=1, source_target_pairs={{0,28},{1,29},{2,30},{3,31},{4,0},{5,1},{6,2},{7,3},{8,4},{9,5},{1... | collective-permute-start | bytes 786440 | tf_op jit(solution)/shard_map/ppermute | solution.py:40
  82.1 9.5 %collective-permute-start.6 = (bf16[2,128,512]{2,1,0:T(8,128)(2,1)S(1)}, bf16[2,128,512]{2,1,0:T(8,128)(2,1)S(1)}, u32[]{:S(2)}, u32[]{:S(2)}) collective-permute-start(bf16[2,128,512]{2,1,0:T(8,128)(2,1)S(1)} %slice.8), channel_id=1, source_target_pairs={{0,4},{1,5},{2,6},{3,7},{4,8},{5,9},{6,10},{7,11},{8,12},{9,13},{1... | collective-permute-start | bytes 786440 | tf_op jit(solution)/shard_map/ppermute | solution.py:40
  91.5 2.2 %copy-start = (bf16[1,1,128,128,128]{4,3,2,1,0:T(8,128)(2,1)S(1)}, bf16[1,1,128,128,128]{4,3,2,1,0:T(8,128)(2,1)}, u32[]{:S(2)}) copy-start(bf16[1,1,128,128,128]{4,3,2,1,0:T(8,128)(2,1)} %param.7) | copy-start | bytes 12582916
  101.7 25.7 %copy-start.1 = (bf16[1,1,128,512]{3,2,1,0:T(8,128)(2,1)S(1)}, bf16[1,1,128,512]{3,2,1,0:T(8,128)(2,1)}, u32[]{:S(2)}) copy-start(bf16[1,1,128,512]{3,2,1,0:T(8,128)(2,1)} %param.11) | copy-start | bytes 393220
  101.7 4.7 %collective-permute-start.11 = (bf16[8,128,512]{2,1,0:T(8,128)(2,1)S(1)}, bf16[8,128,512]{2,1,0:T(8,128)(2,1)S(1)}, u32[]{:S(2)}, u32[]{:S(2)}) collective-permute-start(bf16[8,128,512]{2,1,0:T(8,128)(2,1)S(1)} %get-tuple-element.8), channel_id=1, source_target_pairs={{0,32},{1,33},{2,34},{3,35},{4,36},{5,37},{6,38},{7,39},{8,40},{9,... | collective-permute-start | bytes 3145736 | tf_op jit(solution)/shard_map/ppermute | solution.py:40

commit v3 on v2

--- a/solution.py
+++ b/solution.py
@@ -40,39 +40,55 @@
     return lax.ppermute(value, AXES, moves(step))
 
 
-def spmm_kernel(first, meta, blocks, *refs):
-    pieces = refs[:-7]
-    keep, away, vals, pan, acc, piece_sem, block_sem = refs[-7:]
+def fetch_kernel(meta, blocks, vals, sem):
+    groups = meta[2 * blocks.shape[0]] // GROUP
+
+    def block_copy(g):
+        part = pl.ds(g * GROUP, GROUP)
+        return pltpu.make_async_copy(blocks.at[part], vals.at[part], sem.at[g])
+
+    @pl.loop(0, groups)
+    def _(g):
+        block_copy(g).start()
+
+    @pl.loop(0, groups)
+    def _(g):
+        block_copy(g).wait()
+
+
+def fetch(meta, values):
+    return pl.pallas_call(
+        fetch_kernel,
+        out_shape=jax.ShapeDtypeStruct(values.shape, values.dtype),
+        in_specs=[pl.BlockSpec(memory_space=pltpu.SMEM), pl.BlockSpec(memory_space=pltpu.HBM)],
+        out_specs=pl.BlockSpec(memory_space=pltpu.VMEM),
+        scratch_shapes=[pltpu.SemaphoreType.DMA((values.shape[0] // GROUP,))],
+        compiler_params=pltpu.CompilerParams(vmem_limit_bytes=16 * 2**20),
+        cost_estimate=pl.CostEstimate(flops=0, bytes_accessed=2 * values.size, transcendentals=0),
+    )(meta, values)
+
+
+def spmm_kernel(first, meta, vals, *refs):
+    pieces = refs[:-5]
+    keep, away, pan, acc, piece_sem = refs[-5:]
     sizes = [piece.shape[0] for piece in pieces]
     starts = [sum(sizes[:k]) for k in range(len(sizes))]
-    slots = blocks.shape[0]
+    slots = vals.shape[0]
     count = meta[2 * slots]
     core = meta[2 * slots + 1]
-    groups = count // GROUP
-
-    def block_copy(g):
-        part = pl.ds(g * GROUP, GROUP)
-        return pltpu.make_async_copy(blocks.at[part], vals.at[part], block_sem.at[g])
-
     def piece_copy(k):
         part = pieces[k].at[:, :, pl.ds(first, pan.shape[2])]
         return pltpu.make_async_copy(part, pan.at[pl.ds(starts[k], sizes[k])], piece_sem.at[k])
 
-    block_copy(0).start()
     for k in range(len(pieces)):
         piece_copy(k).start()
-
-    @pl.loop(1, groups)
-    def _(g):
-        block_copy(g).start()
 
     acc[...] = jnp.zeros_like(acc)
     for k in range(len(pieces)):
         piece_copy(k).wait()
 
-    @pl.loop(0, groups)
+    @pl.loop(0, count // GROUP)
     def _(g):
-        block_copy(g).wait()
         for s in range(GROUP):
             slot = g * GROUP + s
             prod = lax.dot_general(
@@ -96,15 +112,13 @@
             jax.ShapeDtypeStruct((blocks_out, bs, width), jnp.float32),
             jax.ShapeDtypeStruct((blocks_out, bs, width), jnp.bfloat16),
         ),
-        in_specs=[pl.BlockSpec(memory_space=pltpu.SMEM), pl.BlockSpec(memory_space=pltpu.HBM)]
+        in_specs=[pl.BlockSpec(memory_space=pltpu.SMEM), pl.BlockSpec(memory_space=pltpu.VMEM)]
         + [anywhere] * len(pieces),
         out_specs=[pl.BlockSpec(memory_space=pltpu.VMEM)] * 2,
         scratch_shapes=[
-            pltpu.VMEM(values.shape, jnp.bfloat16),
             pltpu.VMEM((Z * YH, bs, width), jnp.bfloat16),
             pltpu.VMEM((blocks_out * CORE, bs, width), jnp.float32),
             pltpu.SemaphoreType.DMA((len(pieces),)),
-            pltpu.SemaphoreType.DMA((slots // GROUP,)),
         ],
         compiler_params=pltpu.CompilerParams(vmem_limit_bytes=32 * 2**20),
         cost_estimate=pl.CostEstimate(
@@ -186,6 +200,7 @@
     width = panel.shape[3] // PARTS
     column = gather_column(panel[0, 0])
     pieces = gather_rings(jnp.stack(column))
+    values = fetch(meta, values)
     parts = [spmm(meta, values, pieces, p * width, width) for p in range(PARTS)]
     terms = [reduce_part(*part) for part in parts]
     return finish(pre_act[0, 0], terms)[None, None]

time: 129 us -> 127 us (0.984)
  the two profiles are of different devices: /device:TPU:32 before, /device:TPU:1 now
where the time goes in v3:
time: 127 us; the launch traced here: 126 us
  starting transfers between devices  56.4 us (44%)
  blocking collectives  33.5 us (26%)
  waiting for transfers between devices  23.9 us (19%)
  Pallas kernels  6.85 us (5%)
  other arithmetic  2.37 us (2%)
  local copies, waits for them, and re-layouts  2.23 us (2%)
    ppermute x12, starting transfers between devices, send(): return lax.ppermute(value, AXES, moves(step))  56.4 us
    all_to_all x1, blocking collectives, reduce_part(): lax.all_to_all(both, 'row', 0, 0, axis_index_groups=groups, tiled=True)  33.5 us
    ppermute x12, waiting for transfers between devices, send(): return lax.ppermute(value, AXES, moves(step))  23.9 us
    pallas_call x1, Pallas kernels, spmm(): pl.pallas_call(functools.partial(spmm_kernel, first), out_shape=(jax.Shap...  5 us
  transfers between devices with their start and end apart: 12, of which 7 were waited for; matrix products, arithmetic and copies ran while one was open for 1% of the time, Pallas kernels for 1%

profile of v3, /device:TPU:1, one launch (start us, length us, event | category | flops | bytes accessed | tf_op | source)
XLA Modules:
  0.0 126.0 jit_solution(191069558907018570)
XLA Ops:
  0.0 6.7 %collective-permute-start.2 = (bf16[128,512]{1,0:T(8,128)(2,1)}, bf16[128,512]{1,0:T(8,128)(2,1)S(1)}, u32[]{:S(2)}, u32[]{:S(2)}) collective-permute-start(bf16[128,512]{1,0:T(8,128)(2,1)} %bitcast.16), channel_id=1, source_target_pairs={{0,3},{1,0},{2,1},{3,2},{4,7},{5,4},{6,5},{7,6},{8,11},{9,8},{10,9... | collective-permute-start | bytes 393224 | tf_op jit(solution)/shard_map/ppermute | solution.py:40
  6.7 3.5 %collective-permute-start.1 = (bf16[128,512]{1,0:T(8,128)(2,1)}, bf16[128,512]{1,0:T(8,128)(2,1)S(1)}, u32[]{:S(2)}, u32[]{:S(2)}) collective-permute-start(bf16[128,512]{1,0:T(8,128)(2,1)} %bitcast.17), channel_id=1, source_target_pairs={{0,2},{1,3},{2,0},{3,1},{4,6},{5,7},{6,4},{7,5},{8,10},{9,11},{10,... | collective-permute-start | bytes 393224 | tf_op jit(solution)/shard_map/ppermute | solution.py:40
  10.2 4.2 %collective-permute-start = (bf16[128,512]{1,0:T(8,128)(2,1)}, bf16[128,512]{1,0:T(8,128)(2,1)S(1)}, u32[]{:S(2)}, u32[]{:S(2)}) collective-permute-start(bf16[128,512]{1,0:T(8,128)(2,1)} %bitcast.18), channel_id=1, source_target_pairs={{0,1},{1,2},{2,3},{3,0},{4,5},{5,6},{6,7},{7,4},{8,9},{9,10},{10,1... | collective-permute-start | bytes 393224 | tf_op jit(solution)/shard_map/ppermute | solution.py:40
  14.5 2.1 %collective-permute-done.1 = bf16[128,512]{1,0:T(8,128)(2,1)S(1)} collective-permute-done((bf16[128,512]{1,0:T(8,128)(2,1)}, bf16[128,512]{1,0:T(8,128)(2,1)S(1)}, u32[]{:S(2)}, u32[]{:S(2)}) %collective-permute-start.1) | collective-permute-done | bytes 131104 | tf_op jit(solution)/shard_map/ppermute | solution.py:40
  16.6 2.5 %collective-permute-done = bf16[128,512]{1,0:T(8,128)(2,1)S(1)} collective-permute-done((bf16[128,512]{1,0:T(8,128)(2,1)}, bf16[128,512]{1,0:T(8,128)(2,1)S(1)}, u32[]{:S(2)}, u32[]{:S(2)}) %collective-permute-start) | collective-permute-done | bytes 131104 | tf_op jit(solution)/shard_map/ppermute | solution.py:40
  19.1 1.0 pad_maximum_fusion.refs_0_
  20.1 11.1 %collective-permute-start.7 = (bf16[4,128,512]{2,1,0:T(8,128)(2,1)S(1)}, bf16[4,128,512]{2,1,0:T(8,128)(2,1)S(1)}, u32[]{:S(2)}, u32[]{:S(2)}) collective-permute-start(bf16[4,128,512]{2,1,0:T(8,128)(2,1)S(1)} %pad_maximum_fusion.refs_0_), channel_id=1, source_target_pairs={{0,28},{1,29},{2,30},{3,31},{4,0},{5,1},{6,2},{7,3},{8,4},{9,5},{1... | collective-permute-start | bytes 1572872 | tf_op jit(solution)/shard_map/ppermute | solution.py:40
  31.1 1.9 %collective-permute-start.3 = (bf16[4,128,512]{2,1,0:T(8,128)(2,1)S(1)}, bf16[4,128,512]{2,1,0:T(8,128)(2,1)S(1)}, u32[]{:S(2)}, u32[]{:S(2)}) collective-permute-start(bf16[4,128,512]{2,1,0:T(8,128)(2,1)S(1)} %pad_maximum_fusion.refs_0_), channel_id=1, source_target_pairs={{0,4},{1,5},{2,6},{3,7},{4,8},{5,9},{6,10},{7,11},{8,12},{9,13},{1... | collective-permute-start | bytes 1572872 | tf_op jit(solution)/shard_map/ppermute | solution.py:40
  33.1 6.2 %collective-permute-done.7.refs_8_ = bf16[4,128,512]{2,1,0:T(8,128)(2,1)S(1)} collective-permute-done((bf16[4,128,512]{2,1,0:T(8,128)(2,1)S(1)}, bf16[4,128,512]{2,1,0:T(8,128)(2,1)S(1)}, u32[]{:S(2)}, u32[]{:S(2)}) %collective-permute-start.7) | collective-permute-done | bytes 524320 | tf_op jit(solution)/shard_map/ppermute | solution.py:40
  39.3 5.3 %collective-permute-start.8 = (bf16[4,128,512]{2,1,0:T(8,128)(2,1)S(1)}, bf16[4,128,512]{2,1,0:T(8,128)(2,1)S(1)}, u32[]{:S(2)}, u32[]{:S(2)}) collective-permute-start(bf16[4,128,512]{2,1,0:T(8,128)(2,1)S(1)} %collective-permute-done.7.refs_8_), channel_id=1, source_target_pairs={{0,28},{1,29},{2,30},{3,31},{4,0},{5,1},{6,2},{7,3},{8,4},{9,5},{1... | collective-permute-start | bytes 1572872 | tf_op jit(solution)/shard_map/ppermute | solution.py:40
  44.6 0.0 collective-permute-done.3.refs_1_
  44.6 1.9 %collective-permute-start.4 = (bf16[4,128,512]{2,1,0:T(8,128)(2,1)S(1)}, bf16[4,128,512]{2,1,0:T(8,128)(2,1)}, u32[]{:S(2)}, u32[]{:S(2)}) collective-permute-start(bf16[4,128,512]{2,1,0:T(8,128)(2,1)S(1)} %collective-permute-done.3.refs_1_), channel_id=1, source_target_pairs={{0,4},{1,5},{2,6},{3,7},{4,8},{5,9},{6,10},{7,11},{8,12},{9,13},{1... | collective-permute-start | bytes 1572872 | tf_op jit(solution)/shard_map/ppermute | solution.py:40
  46.5 5.3 %collective-permute-done.8.refs_7_ = bf16[4,128,512]{2,1,0:T(8,128)(2,1)S(1)} collective-permute-done((bf16[4,128,512]{2,1,0:T(8,128)(2,1)S(1)}, bf16[4,128,512]{2,1,0:T(8,128)(2,1)S(1)}, u32[]{:S(2)}, u32[]{:S(2)}) %collective-permute-start.8) | collective-permute-done | bytes 524320 | tf_op jit(solution)/shard_map/ppermute | solution.py:40
  51.8 5.3 %collective-permute-start.9 = (bf16[4,128,512]{2,1,0:T(8,128)(2,1)S(1)}, bf16[4,128,512]{2,1,0:T(8,128)(2,1)S(1)}, u32[]{:S(2)}, u32[]{:S(2)}) collective-permute-start(bf16[4,128,512]{2,1,0:T(8,128)(2,1)S(1)} %collective-permute-done.8.refs_7_), channel_id=1, source_target_pairs={{0,28},{1,29},{2,30},{3,31},{4,0},{5,1},{6,2},{7,3},{8,4},{9,5},{1... | collective-permute-start | bytes 1572872 | tf_op jit(solution)/shard_map/ppermute | solution.py:40
  57.1 0.0 collective-permute-done.4.refs_2_
  57.2 1.9 %collective-permute-start.5 = (bf16[4,128,512]{2,1,0:T(8,128)(2,1)}, bf16[4,128,512]{2,1,0:T(8,128)(2,1)S(1)}, u32[]{:S(2)}, u32[]{:S(2)}) collective-permute-start(bf16[4,128,512]{2,1,0:T(8,128)(2,1)} %collective-permute-done.4.refs_2_), channel_id=1, source_target_pairs={{0,4},{1,5},{2,6},{3,7},{4,8},{5,9},{6,10},{7,11},{8,12},{9,13},{1... | collective-permute-start | bytes 1572872 | tf_op jit(solution)/shard_map/ppermute | solution.py:40
  59.7 3.5 %collective-permute-done.9.refs_6_ = bf16[4,128,512]{2,1,0:T(8,128)(2,1)S(1)} collective-permute-done((bf16[4,128,512]{2,1,0:T(8,128)(2,1)S(1)}, bf16[4,128,512]{2,1,0:T(8,128)(2,1)S(1)}, u32[]{:S(2)}, u32[]{:S(2)}) %collective-permute-start.9) | collective-permute-done | bytes 524320 | tf_op jit(solution)/shard_map/ppermute | solution.py:40
  63.3 5.5 %collective-permute-start.10 = (bf16[2,128,512]{2,1,0:T(8,128)(2,1)S(1)}, bf16[2,128,512]{2,1,0:T(8,128)(2,1)S(1)}, u32[]{:S(2)}, u32[]{:S(2)}) collective-permute-start(bf16[2,128,512]{2,1,0:T(8,128)(2,1)S(1)} %slice.9), channel_id=1, source_target_pairs={{0,28},{1,29},{2,30},{3,31},{4,0},{5,1},{6,2},{7,3},{8,4},{9,5},{1... | collective-permute-start | bytes 786440 | tf_op jit(solution)/shard_map/ppermute | solution.py:40
  68.8 0.0 collective-permute-done.5.refs_3_
  68.8 1.9 %collective-permute-start.6 = (bf16[2,128,512]{2,1,0:T(8,128)(2,1)S(1)}, bf16[2,128,512]{2,1,0:T(8,128)(2,1)S(1)}, u32[]{:S(2)}, u32[]{:S(2)}) collective-permute-start(bf16[2,128,512]{2,1,0:T(8,128)(2,1)S(1)} %slice.8), channel_id=1, source_target_pairs={{0,4},{1,5},{2,6},{3,7},{4,8},{5,9},{6,10},{7,11},{8,12},{9,13},{1... | collective-permute-start | bytes 786440 | tf_op jit(solution)/shard_map/ppermute | solution.py:40
  70.8 0.7 add_bitcast_fusion
  71.4 0.7 pad_add_fusion.meta
  72.2 2.2 %copy-done = bf16[1,1,128,128,128]{4,3,2,1,0:T(8,128)(2,1)S(1)} copy-done((bf16[1,1,128,128,128]{4,3,2,1,0:T(8,128)(2,1)S(1)}, bf16[1,1,128,128,128]{4,3,2,1,0:T(8,128)(2,1)}, u32[]{:S(2)}) %copy-start) | copy-done | bytes 4194328
  74.3 0.8 shard_map.64.vals
  75.2 2.0 %collective-permute-done.6.refs_4_ = bf16[2,128,512]{2,1,0:T(8,128)(2,1)S(1)} collective-permute-done((bf16[2,128,512]{2,1,0:T(8,128)(2,1)S(1)}, bf16[2,128,512]{2,1,0:T(8,128)(2,1)S(1)}, u32[]{:S(2)}, u32[]{:S(2)}) %collective-permute-start.6) | collective-permute-done | bytes 262176 | tf_op jit(solution)/shard_map/ppermute | solution.py:40
  77.2 5.0 %shard_map.65 = (f32[8,128,512]{2,1,0:T(8,128)S(1)}, bf16[8,128,512]{2,1,0:T(8,128)(2,1)S(1)}) custom-call(s32[258]{0:T(512)S(1)} %pad_add_fusion.meta, bf16[128,128,128]{2,1,0:T(8,128)(2,1)S(1)} %shard_map.64.vals, bf16[4,128,512]{2,1,0:T(8,128)(2,1)S(1)} %pad_maximum_fusion.refs_0_, bf16[4,128,512]{2,1,0:T(8,128)(2,1)S(1)} %collective-permute-done.3.refs_1_, ...), custom_call_target="tpu_custom_call" | custom-call | flops 2147483648 | bytes 8388608 | tf_op jit(solution)/shard_map/pallas_call | solution.py:109
  82.2 0.0 copy-start.1
  82.2 7.0 %collective-permute-start.11 = (bf16[8,128,512]{2,1,0:T(8,128)(2,1)S(1)}, bf16[8,128,512]{2,1,0:T(8,128)(2,1)S(1)}, u32[]{:S(2)}, u32[]{:S(2)}) collective-permute-start(bf16[8,128,512]{2,1,0:T(8,128)(2,1)S(1)} %get-tuple-element.8), channel_id=1, source_target_pairs={{0,32},{1,33},{2,34},{3,35},{4,36},{5,37},{6,38},{7,39},{8,40},{9,... | collective-permute-start | bytes 3145736 | tf_op jit(solution)/shard_map/ppermute | solution.py:40
  89.2 2.3 %collective-permute-done.11.came = bf16[8,128,512]{2,1,0:T(8,128)(2,1)S(1)} collective-permute-done((bf16[8,128,512]{2,1,0:T(8,128)(2,1)S(1)}, bf16[8,128,512]{2,1,0:T(8,128)(2,1)S(1)}, u32[]{:S(2)}, u32[]{:S(2)}) %collective-permute-start.11) | collective-permute-done | bytes 1048608 | tf_op jit(solution)/shard_map/ppermute | solution.py:40
  91.5 0.2 shard_map.66
  91.7 33.5 %all_to_all.5.refs_0_ = bf16[8,128,512]{2,1,0:T(8,128)(2,1)S(1)} all-to-all(bf16[8,128,512]{2,1,0:T(8,128)(2,1)S(1)} %shard_map.66), channel_id=1, replica_groups={{0,64,128,192,256,320,384,448},{32,96,160,224,288,352,416,480},{1,65,12..., dimensions={0} | all-to-all | bytes 2097152 | tf_op jit(solution)/shard_map/all_to_all | solution.py:188
  125.2 0.8 shard_map.67
  (6 shorter events, 0.0 us)
Async XLA Ops:
  0.0 14.5 %collective-permute-start.2 = (bf16[128,512]{1,0:T(8,128)(2,1)}, bf16[128,512]{1,0:T(8,128)(2,1)S(1)}, u32[]{:S(2)}, u32[]{:S(2)}) collective-permute-start(bf16[128,512]{1,0:T(8,128)(2,1)} %bitcast.16), channel_id=1, source_target_pairs={{0,3},{1,0},{2,1},{3,2},{4,7},{5,4},{6,5},{7,6},{8,11},{9,8},{10,9... | collective-permute-start | bytes 393224 | tf_op jit(solution)/shard_map/ppermute | solution.py:40
  6.7 9.9 %collective-permute-start.1 = (bf16[128,512]{1,0:T(8,128)(2,1)}, bf16[128,512]{1,0:T(8,128)(2,1)S(1)}, u32[]{:S(2)}, u32[]{:S(2)}) collective-permute-start(bf16[128,512]{1,0:T(8,128)(2,1)} %bitcast.17), channel_id=1, source_target_pairs={{0,2},{1,3},{2,0},{3,1},{4,6},{5,7},{6,4},{7,5},{8,10},{9,11},{10,... | collective-permute-start | bytes 393224 | tf_op jit(solution)/shard_map/ppermute | solution.py:40
  10.2 8.8 %collective-permute-start = (bf16[128,512]{1,0:T(8,128)(2,1)}, bf16[128,512]{1,0:T(8,128)(2,1)S(1)}, u32[]{:S(2)}, u32[]{:S(2)}) collective-permute-start(bf16[128,512]{1,0:T(8,128)(2,1)} %bitcast.18), channel_id=1, source_target_pairs={{0,1},{1,2},{2,3},{3,0},{4,5},{5,6},{6,7},{7,4},{8,9},{9,10},{10,1... | collective-permute-start | bytes 393224 | tf_op jit(solution)/shard_map/ppermute | solution.py:40
  20.1 19.2 %collective-permute-start.7 = (bf16[4,128,512]{2,1,0:T(8,128)(2,1)S(1)}, bf16[4,128,512]{2,1,0:T(8,128)(2,1)S(1)}, u32[]{:S(2)}, u32[]{:S(2)}) collective-permute-start(bf16[4,128,512]{2,1,0:T(8,128)(2,1)S(1)} %pad_maximum_fusion.refs_0_), channel_id=1, source_target_pairs={{0,28},{1,29},{2,30},{3,31},{4,0},{5,1},{6,2},{7,3},{8,4},{9,5},{1... | collective-permute-start | bytes 1572872 | tf_op jit(solution)/shard_map/ppermute | solution.py:40
  31.1 13.5 %collective-permute-start.3 = (bf16[4,128,512]{2,1,0:T(8,128)(2,1)S(1)}, bf16[4,128,512]{2,1,0:T(8,128)(2,1)S(1)}, u32[]{:S(2)}, u32[]{:S(2)}) collective-permute-start(bf16[4,128,512]{2,1,0:T(8,128)(2,1)S(1)} %pad_maximum_fusion.refs_0_), channel_id=1, source_target_pairs={{0,4},{1,5},{2,6},{3,7},{4,8},{5,9},{6,10},{7,11},{8,12},{9,13},{1... | collective-permute-start | bytes 1572872 | tf_op jit(solution)/shard_map/ppermute | solution.py:40
  39.3 12.5 %collective-permute-start.8 = (bf16[4,128,512]{2,1,0:T(8,128)(2,1)S(1)}, bf16[4,128,512]{2,1,0:T(8,128)(2,1)S(1)}, u32[]{:S(2)}, u32[]{:S(2)}) collective-permute-start(bf16[4,128,512]{2,1,0:T(8,128)(2,1)S(1)} %collective-permute-done.7.refs_8_), channel_id=1, source_target_pairs={{0,28},{1,29},{2,30},{3,31},{4,0},{5,1},{6,2},{7,3},{8,4},{9,5},{1... | collective-permute-start | bytes 1572872 | tf_op jit(solution)/shard_map/ppermute | solution.py:40
  44.6 12.5 %collective-permute-start.4 = (bf16[4,128,512]{2,1,0:T(8,128)(2,1)S(1)}, bf16[4,128,512]{2,1,0:T(8,128)(2,1)}, u32[]{:S(2)}, u32[]{:S(2)}) collective-permute-start(bf16[4,128,512]{2,1,0:T(8,128)(2,1)S(1)} %collective-permute-done.3.refs_1_), channel_id=1, source_target_pairs={{0,4},{1,5},{2,6},{3,7},{4,8},{5,9},{6,10},{7,11},{8,12},{9,13},{1... | collective-permute-start | bytes 1572872 | tf_op jit(solution)/shard_map/ppermute | solution.py:40
  51.8 11.4 %collective-permute-start.9 = (bf16[4,128,512]{2,1,0:T(8,128)(2,1)S(1)}, bf16[4,128,512]{2,1,0:T(8,128)(2,1)S(1)}, u32[]{:S(2)}, u32[]{:S(2)}) collective-permute-start(bf16[4,128,512]{2,1,0:T(8,128)(2,1)S(1)} %collective-permute-done.8.refs_7_), channel_id=1, source_target_pairs={{0,28},{1,29},{2,30},{3,31},{4,0},{5,1},{6,2},{7,3},{8,4},{9,5},{1... | collective-permute-start | bytes 1572872 | tf_op jit(solution)/shard_map/ppermute | solution.py:40
  57.2 11.6 %collective-permute-start.5 = (bf16[4,128,512]{2,1,0:T(8,128)(2,1)}, bf16[4,128,512]{2,1,0:T(8,128)(2,1)S(1)}, u32[]{:S(2)}, u32[]{:S(2)}) collective-permute-start(bf16[4,128,512]{2,1,0:T(8,128)(2,1)} %collective-permute-done.4.refs_2_), channel_id=1, source_target_pairs={{0,4},{1,5},{2,6},{3,7},{4,8},{5,9},{6,10},{7,11},{8,12},{9,13},{1... | collective-permute-start | bytes 1572872 | tf_op jit(solution)/shard_map/ppermute | solution.py:40
  63.3 11.9 %collective-permute-start.10 = (bf16[2,128,512]{2,1,0:T(8,128)(2,1)S(1)}, bf16[2,128,512]{2,1,0:T(8,128)(2,1)S(1)}, u32[]{:S(2)}, u32[]{:S(2)}) collective-permute-start(bf16[2,128,512]{2,1,0:T(8,128)(2,1)S(1)} %slice.9), channel_id=1, source_target_pairs={{0,28},{1,29},{2,30},{3,31},{4,0},{5,1},{6,2},{7,3},{8,4},{9,5},{1... | collective-permute-start | bytes 786440 | tf_op jit(solution)/shard_map/ppermute | solution.py:40
  68.8 8.3 %collective-permute-start.6 = (bf16[2,128,512]{2,1,0:T(8,128)(2,1)S(1)}, bf16[2,128,512]{2,1,0:T(8,128)(2,1)S(1)}, u32[]{:S(2)}, u32[]{:S(2)}) collective-permute-start(bf16[2,128,512]{2,1,0:T(8,128)(2,1)S(1)} %slice.8), channel_id=1, source_target_pairs={{0,4},{1,5},{2,6},{3,7},{4,8},{5,9},{6,10},{7,11},{8,12},{9,13},{1... | collective-permute-start | bytes 786440 | tf_op jit(solution)/shard_map/ppermute | solution.py:40
  72.2 2.2 %copy-start = (bf16[1,1,128,128,128]{4,3,2,1,0:T(8,128)(2,1)S(1)}, bf16[1,1,128,128,128]{4,3,2,1,0:T(8,128)(2,1)}, u32[]{:S(2)}) copy-start(bf16[1,1,128,128,128]{4,3,2,1,0:T(8,128)(2,1)} %param.7) | copy-start | bytes 12582916
  82.2 43.0 %copy-start.1 = (bf16[1,1,128,512]{3,2,1,0:T(8,128)(2,1)S(1)}, bf16[1,1,128,512]{3,2,1,0:T(8,128)(2,1)}, u32[]{:S(2)}) copy-start(bf16[1,1,128,512]{3,2,1,0:T(8,128)(2,1)} %param.11) | copy-start | bytes 393220
  82.2 9.3 %collective-permute-start.11 = (bf16[8,128,512]{2,1,0:T(8,128)(2,1)S(1)}, bf16[8,128,512]{2,1,0:T(8,128)(2,1)S(1)}, u32[]{:S(2)}, u32[]{:S(2)}) collective-permute-start(bf16[8,128,512]{2,1,0:T(8,128)(2,1)S(1)} %get-tuple-element.8), channel_id=1, source_target_pairs={{0,32},{1,33},{2,34},{3,35},{4,36},{5,37},{6,38},{7,39},{8,40},{9,... | collective-permute-start | bytes 3145736 | tf_op jit(solution)/shard_map/ppermute | solution.py:40
